TPU v7x, 768 devices: a whole 4x8x12 slice. The times are simulated.
768 devices in a mesh: nodes: 16 (over y, x_lo), feat: 48 (over x_hi, z, core).
Axes of the slice: x: 4 (x_hi: 2, x_lo: 2; x = x_hi * 2 + x_lo), y: 8, z: 12, core: 2. Of those that a mesh axis runs over, the one named last changes fastest.
Arguments:
- features: bfloat16 [98304, 256], P(('feat', 'nodes')), may hold values from -6 to 6
- weight: bfloat16 [256, 256], replicated, may hold values from -0.375 to 0.375
- tiles: bfloat16 [36864, 128, 128], P(('nodes', 'feat')), may hold values from -0.078125 to 0.078125
- tile_rows: int32 [36864], P(('nodes', 'feat')), may hold values from 0 to 47
- tile_cols: int32 [36864], P(('nodes', 'feat')), may hold values from 0 to 15
- live: int32 [768], P(('nodes', 'feat')), may hold values from 24 to 48, as said below
- cotangent: bfloat16 [98304, 256], P(('nodes', 'feat')), may hold values from -6 to 6
Outputs:
- output: bfloat16 [98304, 256], P(('nodes', 'feat'))
- feature_grad: bfloat16 [98304, 256], P(('feat', 'nodes'))
- weight_grad: float32 [256, 256], replicated
Inputs may be any that keep to these rules, and one draw needn't show every extreme that they name: `live`: some block uses all 48 slots.
All inputs are finite; a program needn't handle non-finite values.
Results may differ from a plain program's by a relative error of at most 0.0049.
Values may be sent and summed in bfloat16 or wider, within the bound.
A program may use at most 64 MiB of HBM per device.

v0:
```python
import math

import jax
import jax.numpy as jnp
from jax import lax
from jax.sharding import PartitionSpec as P


def selector(index_values, count):
    places = jnp.arange(count, dtype=jnp.int32)
    return (index_values[:, None] == places[None, :]).astype(jnp.float32)


def fetch_tiles(whole, pick, tile_side):
    stacked = whole.reshape(whole.shape[0] // tile_side, tile_side, whole.shape[1])
    pulled = jnp.einsum(
        "kt,taf->kaf", pick.astype(jnp.bfloat16), stacked, preferred_element_type=jnp.float32
    )
    return pulled.astype(jnp.bfloat16)


def place_tiles(terms, place, tile_side):
    placed = jnp.einsum("tk,kaf->taf", place, terms, precision=lax.Precision.HIGHEST)
    return placed.reshape(place.shape[0] * tile_side, terms.shape[2])


def body(features, weight, tiles, tile_rows, tile_cols, live, cotangent):
    slot_count = tiles.shape[0]
    tile_side = tiles.shape[1]
    nodes_total = features.shape[0] * lax.axis_size("nodes") * lax.axis_size("feat")
    row_tiles = features.shape[0] * lax.axis_size("feat") // tile_side
    col_tiles = features.shape[0] * lax.axis_size("nodes") // tile_side
    live_mask = (jnp.arange(slot_count, dtype=jnp.int32) < live[0]).astype(jnp.float32)
    row_pick = selector(tile_rows, row_tiles)
    col_pick = selector(tile_cols, col_tiles)
    row_place = (row_pick * live_mask[:, None]).T
    col_place = (col_pick * live_mask[:, None]).T
    panel = lax.all_gather(features, "nodes", axis=0, tiled=True)
    pulled = fetch_tiles(panel, col_pick, tile_side)
    products = jnp.einsum("kab,kbf->kaf", tiles, pulled, preferred_element_type=jnp.float32)
    partial_value = place_tiles(products, row_place, tile_side)
    aggregate = lax.psum_scatter(partial_value, "feat", scatter_dimension=0, tiled=True).astype(
        jnp.bfloat16
    )
    output = jnp.dot(aggregate, weight, preferred_element_type=jnp.float32).astype(jnp.bfloat16)
    cotangent_whole = lax.all_gather(cotangent, "feat", axis=0, tiled=True)
    grad_whole = jnp.dot(cotangent_whole, weight.T, preferred_element_type=jnp.float32).astype(
        jnp.bfloat16
    )
    gathered = fetch_tiles(grad_whole, row_pick, tile_side)
    back_terms = jnp.einsum("kab,kaf->kbf", tiles, gathered, preferred_element_type=jnp.float32)
    panel_part = place_tiles(back_terms, col_place, tile_side)
    feature_grad = lax.psum_scatter(panel_part, "nodes", scatter_dimension=0, tiled=True).astype(
        jnp.bfloat16
    )
    local_term = jnp.dot(aggregate.T, cotangent, preferred_element_type=jnp.float32)
    weight_grad = lax.psum(local_term, ("nodes", "feat")) * (1.0 / math.sqrt(nodes_total))
    return (output, feature_grad, weight_grad)


def solution(mesh):
    in_specs = (
        P(("feat", "nodes"), None),
        P(),
        P(("nodes", "feat"), None, None),
        P(("nodes", "feat")),
        P(("nodes", "feat")),
        P(("nodes", "feat")),
        P(("nodes", "feat"), None),
    )
    out_specs = (P(("nodes", "feat"), None), P(("feat", "nodes"), None), P())
    return jax.shard_map(body, mesh=mesh, in_specs=in_specs, out_specs=out_specs, check_vma=False)
```

profile of v0, /device:TPU:1, one launch (start us, length us, event | category | flops | bytes accessed | tf_op | source)
XLA Modules:
  0.0 970.2 jit_solution(973186163202118286)
XLA Ops:
  7.2 0.0 copy-start
  7.2 0.0 all-gather.5.cloned.1.call-start
  7.2 0.7 all-gather.5.cloned.1.call-update
  7.9 0.0 all-gather.3.cloned.1.call-start
  8.0 0.7 all-gather.3.cloned.1.call-update
  8.7 0.0 reduce-scatter.5.cloned.1.call-start
  9.4 0.0 copy-start.4
  9.4 133.1 %all-gather.5.cloned.1.call-done = bf16[6144,256]{1,0:T(8,128)(2,1)} async-done(((bf16[128,256]{1,0:T(8,128)(2,1)}), bf16[6144,256]{1,0:T(8,128)(2,1)}) %all-gather.5.cloned.1.call-update) | async-done | bytes 3145744 | tf_op jit(solution)/shard_map/all_gather | solution.py:46
  142.4 2.9 convolution_convert_fusion
  145.3 0.0 copy-done.4
  145.4 2.6 fusion.6
  147.9 0.0 copy-done
  148.0 4.0 fusion.5
  151.9 0.0 copy-start.3
  151.9 6.7 copy.17
  158.6 0.0 copy-done.3
  158.6 5.1 fusion
  163.7 2.5 copy.11
  166.3 0.0 reduce-scatter.5.cloned.1.call-update
  166.3 0.2 reduce-scatter.3.cloned.1.call-start
  166.5 38.2 %all-gather.3.cloned.1.call-done = bf16[2048,256]{1,0:T(8,128)(2,1)} async-done(((bf16[128,256]{1,0:T(8,128)(2,1)}), bf16[2048,256]{1,0:T(8,128)(2,1)}) %all-gather.3.cloned.1.call-update) | async-done | bytes 1048592 | tf_op jit(solution)/shard_map/all_gather | solution.py:38
  204.8 2.2 fusion.8
  207.0 3.9 fusion.4
  210.9 6.6 copy.14
  217.6 7.7 fusion.2
  225.2 6.3 copy.10
  231.5 0.0 copy-start.2
  231.5 0.0 copy-start.1
  231.5 0.0 reduce-scatter.3.cloned.1.call-update
  231.6 0.0 all-reduce.2.cloned.1.call-start
  231.6 55.8 %reduce-scatter.5.cloned.1.call-done = f32[128,256]{1,0:T(8,128)} async-done(((f32[2048,256]{1,0:T(8,128)}), f32[128,256]{1,0:T(8,128)}) %reduce-scatter.5.cloned.1.call-update) | async-done | bytes 131088 | tf_op jit(solution)/shard_map/reduce_scatter | solution.py:53
  287.5 1.5 convert_element_type.47
  289.0 199.8 %reduce-scatter.3.cloned.1.call-done = f32[128,256]{1,0:T(8,128)} async-done(((f32[6144,256]{1,0:T(8,128)}), f32[128,256]{1,0:T(8,128)}) %reduce-scatter.3.cloned.1.call-update) | async-done | bytes 131088 | tf_op jit(solution)/shard_map/reduce_scatter | solution.py:42
  488.8 0.0 copy-done.2
  488.8 1.8 fusion.10
  490.6 0.0 all-reduce.2.cloned.1.call-update
  490.6 0.0 copy-done.1
  490.6 1.7 convolution_convert_fusion.1
  492.3 469.6 %all-reduce.2.cloned.1.call-done = f32[256,256]{1,0:T(8,128)} async-done(((f32[256,256]{1,0:T(8,128)}), f32[256,256]{1,0:T(8,128)}) %all-reduce.2.cloned.1.call-update) | async-done | bytes 262160 | tf_op jit(solution)/shard_map/psum | solution.py:57
  961.9 1.7 broadcast_multiply_fusion
  (1 shorter events, 0.0 us)
Async XLA Ops:
  7.2 140.8 %copy-start = (bf16[48,128,128]{2,1,0:T(8,128)(2,1)S(1)}, bf16[48,128,128]{2,1,0:T(8,128)(2,1)}, u32[]{:S(2)}) copy-start(bf16[48,128,128]{2,1,0:T(8,128)(2,1)} %param.9) | copy-start | bytes 4718596
  7.2 135.3 %all-gather.5.cloned.1.call-start = ((), (), s32[]{:S(2)}) async-start(), calls=%async_computation.4 | async-start | bytes 3211264 | tf_op jit(solution)/shard_map/all_gather | solution.py:46
  7.9 196.9 %all-gather.3.cloned.1.call-start = ((), (), s32[]{:S(2)}) async-start(), calls=%async_computation.2 | async-start | bytes 1114112 | tf_op jit(solution)/shard_map/all_gather | solution.py:38
  8.7 278.8 %reduce-scatter.5.cloned.1.call-start = ((), (), s32[]{:S(2)}) async-start(), calls=%async_computation.5 | async-start | bytes 2228224 | tf_op jit(solution)/shard_map/reduce_scatter | solution.py:53
  9.4 136.0 %copy-start.4 = (s32[48]{0:T(128)S(1)}, s32[48]{0:T(128)}, u32[]{:S(2)}) copy-start(s32[48]{0:T(128)} %param.10) | copy-start | bytes 580
  151.9 6.7 copy-start.3
  166.3 322.5 %reduce-scatter.3.cloned.1.call-start = ((), (), s32[]{:S(2)}) async-start(), calls=%async_computation.3 | async-start | bytes 6422528 | tf_op jit(solution)/shard_map/reduce_scatter | solution.py:42
  231.5 257.2 %copy-start.2 = (bf16[128,256]{1,0:T(8,128)(2,1)S(1)}, bf16[128,256]{1,0:T(8,128)(2,1)}, u32[]{:S(2)}) copy-start(bf16[128,256]{1,0:T(8,128)(2,1)} %param.13) | copy-start | bytes 196612
  231.5 259.1 %copy-start.1 = (bf16[256,256]{1,0:T(8,128)(2,1)S(1)}, bf16[256,256]{1,0:T(8,128)(2,1)}, u32[]{:S(2)}) copy-start(bf16[256,256]{1,0:T(8,128)(2,1)} %param.8) | copy-start | bytes 393220
  231.6 730.4 %all-reduce.2.cloned.1.call-start = ((), (), s32[]{:S(2)}) async-start(), calls=%async_computation.6 | async-start | bytes 524288 | tf_op jit(solution)/shard_map/psum | solution.py:57
Sparse Core Ops, SparseCore 0:
  11.7 130.6 all-gather.4
  144.8 59.9 all-gather.2
  207.9 79.5 reduce-scatter.4
  292.7 196.0 reduce-scatter.2
  494.6 467.2 all-reduce.1
where the time goes:
time: 970 us
  waiting for transfers between devices  898 us (93%)
  matrix products  32 us (3%)
  local copies, waits for them, and re-layouts  22.2 us (2%)
  between operations  14.5 us (1%)
    psum x1, waiting for transfers between devices, body(): lax.psum(local_term, ('nodes', 'feat')) * (1.0 / math.sqrt(nodes_total))  470 us
    reduce_scatter x1, waiting for transfers between devices, body(): lax.psum_scatter(partial_value, 'feat', scatter_dimension=0, tiled=True)  200 us
    all_gather x1, waiting for transfers between devices, body(): cotangent_whole = lax.all_gather(cotangent, 'feat', axis=0, tiled=True)  133 us
    reduce_scatter x1, waiting for transfers between devices, body(): lax.psum_scatter(panel_part, 'nodes', scatter_dimension=0, tiled=True)  55.8 us
    all_gather x1, waiting for transfers between devices, body(): panel = lax.all_gather(features, 'nodes', axis=0, tiled=True)  38.2 us
  transfers between devices with their start and end apart: 5, of which 5 were waited for; matrix products, arithmetic and copies ran while one was open for 6% of the time, Pallas kernels for 0%

commit v1 on v0

v1 whole, which is shorter than its diff:
```python
import functools
import math

import jax
import jax.numpy as jnp
from jax import lax
from jax.experimental import pallas as pl
from jax.experimental.pallas import tpu as pltpu
from jax.sharding import PartitionSpec as P

MESH = pl.DeviceIdType.MESH
VMEM = pl.BlockSpec(memory_space=pltpu.VMEM)
SMEM = pl.BlockSpec(memory_space=pltpu.SMEM)
LIMIT = 40 * 1024 * 1024
PAIR = 2


class Place:
    def __init__(self, n_nodes, n_feat):
        self.n_nodes, self.n_feat = n_nodes, n_feat
        self.ny, self.nz = n_nodes // PAIR, n_feat // (PAIR * PAIR)
        self.i, self.j = lax.axis_index("nodes"), lax.axis_index("feat")
        self.y, self.xl = lax.div(self.i, PAIR), lax.rem(self.i, PAIR)
        self.xh = lax.div(self.j, PAIR * self.nz)
        self.z = lax.rem(lax.div(self.j, PAIR), self.nz)
        self.core = lax.rem(self.j, PAIR)

    def node(self, y, xl):
        return y * PAIR + xl

    def feat(self, xh, z, core):
        return (xh * self.nz + z) * PAIR + core


def greet(partners):
    barrier = pltpu.get_barrier_semaphore()
    for device in partners:
        pl.semaphore_signal(barrier, inc=1, device_id=device, device_id_type=MESH)
    pl.semaphore_wait(barrier, len(partners))


def remote(src, dst, send_sem, recv_sem, device):
    return pltpu.make_async_remote_copy(
        src_ref=src, dst_ref=dst, send_sem=send_sem, recv_sem=recv_sem, device_id=device, device_id_type=MESH
    )


def gather_kernel(
    n_nodes, n_feat, x_ref, c_ref, x_all, c_all, xs, xr, zs, zr, cs, cr, ls, lr, ys, yr
):
    at = Place(n_nodes, n_feat)
    nz, ny = at.nz, at.ny
    z_near = [lax.rem(at.z + 1, nz), lax.rem(at.z + nz - 1, nz)]
    y_near = [lax.rem(at.y + 1, ny), lax.rem(at.y + ny - 1, ny)]
    sibling = (at.i, at.feat(at.xh, at.z, 1 - at.core))
    across = (at.i, at.feat(1 - at.xh, at.z, at.core))
    beside = (at.node(at.y, 1 - at.xl), at.j)
    along_z = [(at.i, at.feat(at.xh, z, at.core)) for z in z_near]
    along_y = [(at.node(y, at.xl), at.j) for y in y_near]
    greet([sibling, across, beside] + along_z + along_y)

    half_z, half_y = nz // 2, ny // 2

    def last_z(s, d):
        return half_z if s == d else nz - 1 - half_z

    def last_y(s, d):
        return half_y if s == d else ny - 1 - half_y

    def origin(place, count, d, t):
        return lax.rem(place + (count - t if d == 0 else t), count)

    def xh_of(s):
        return at.xh if s == 0 else 1 - at.xh

    def xl_of(s):
        return at.xl if s == 0 else 1 - at.xl

    def z_copy(s, d, t, origin_z):
        block = c_all.at[at.feat(xh_of(s), origin_z, at.core)]
        src = c_ref if (s == 0 and t == 1) else block
        return remote(src, block, zs.at[s, d, t - 1], zr.at[s, d, t - 1], along_z[d])

    def sibling_copy(s, origin_z, src=None, arriving=False):
        core = 1 - at.core if arriving else at.core
        block = c_all.at[at.feat(xh_of(s), origin_z, core)]
        k = s * nz + origin_z
        return remote(block if src is None else src, block, cs.at[k], cr.at[k], sibling)

    def y_copy(s, d, t, origin_y):
        block = x_all.at[at.node(origin_y, xl_of(s))]
        src = x_ref if (s == 0 and t == 1) else block
        return remote(src, block, ys.at[s, d, t - 1], yr.at[s, d, t - 1], along_y[d])

    z_sent, y_sent = [], []

    def z_start(s, d, t):
        copy = z_copy(s, d, t, origin(at.z, nz, d, t - 1))
        copy.start()
        z_sent.append(copy)

    def y_start(s, d, t):
        copy = y_copy(s, d, t, origin(at.y, ny, d, t - 1))
        copy.start()
        y_sent.append(copy)

    def across_copy(xh):
        return remote(c_ref, c_all.at[at.feat(xh, at.z, at.core)], xs, xr, across)

    def beside_copy(xl):
        return remote(x_ref, x_all.at[at.node(at.y, xl)], ls, lr, beside)

    across_copy(at.xh).start()
    beside_copy(at.xl).start()
    for d in (0, 1):
        z_start(0, d, 1)
        y_start(0, d, 1)
    sent_over = [sibling_copy(0, at.z, c_ref)]
    sent_over[0].start()
    c_all[at.j] = c_ref[...]
    x_all[at.i] = x_ref[...]
    beside_copy(1 - at.xl).wait_recv()
    for d in (0, 1):
        y_start(1, d, 1)
    across_copy(1 - at.xh).wait_recv()
    for d in (0, 1):
        z_start(1, d, 1)
    copy = sibling_copy(1, at.z)
    copy.start()
    sent_over.append(copy)

    for t in range(1, half_z + 1):
        for s in (0, 1):
            for d in (0, 1):
                if t <= last_y(s, d):
                    y_copy(s, d, t, origin(at.y, ny, d, t)).wait_recv()
                    if t < last_y(s, d):
                        y_start(s, d, t + 1)
                if t <= last_z(s, d):
                    origin_z = origin(at.z, nz, d, t)
                    z_copy(s, d, t, origin_z).wait_recv()
                    if t < last_z(s, d):
                        z_start(s, d, t + 1)
                    copy = sibling_copy(s, origin_z)
                    copy.start()
                    sent_over.append(copy)
    for s in (0, 1):
        for z in range(nz):
            sibling_copy(s, z, arriving=True).wait_recv()
    for copy in sent_over + z_sent + y_sent:
        copy.wait_send()
    across_copy(at.xh).wait_send()
    beside_copy(at.xl).wait_send()


def gather(n_nodes, n_feat, features, cotangent):
    rows, width = features.shape
    ny, nz = n_nodes // PAIR, n_feat // (PAIR * PAIR)
    dma = pltpu.SemaphoreType.DMA
    return pl.pallas_call(
        functools.partial(gather_kernel, n_nodes, n_feat),
        out_shape=(
            jax.ShapeDtypeStruct((n_nodes, rows, width), features.dtype),
            jax.ShapeDtypeStruct((n_feat, rows, width), cotangent.dtype),
        ),
        in_specs=[VMEM, VMEM],
        out_specs=(VMEM, VMEM),
        scratch_shapes=[
            dma,
            dma,
            dma((2, 2, nz // 2)),
            dma((2, 2, nz // 2)),
            dma((2 * nz,)),
            dma((2 * nz,)),
            dma,
            dma,
            dma((2, 2, ny // 2)),
            dma((2, 2, ny // 2)),
        ],
        compiler_params=pltpu.CompilerParams(collective_id=0, has_side_effects=True, vmem_limit_bytes=LIMIT),
        name="gather_blocks",
    )(features, cotangent)


def sparse_kernel(group, rows, cols, live, tiles, x_all, c_all, p_out, b_out, w_out, p_sum, b_sum):
    n_feat = p_out.shape[0]
    n_nodes = x_all.shape[0]

    def clear_p(r, carry):
        p_sum[r] = jnp.zeros(p_sum.shape[1:], jnp.float32)
        return carry

    def clear_b(c, carry):
        b_sum[c] = jnp.zeros(b_sum.shape[1:], jnp.float32)
        return carry

    lax.fori_loop(0, n_feat, clear_p, 0)
    lax.fori_loop(0, n_nodes, clear_b, 0)
    used = live[0]

    def step(g, carry):
        terms = []
        for u in range(group):
            k = g * group + u
            r, c = rows[k], cols[k]
            tile = tiles[k]
            ahead = jnp.dot(tile, x_all[c], preferred_element_type=jnp.float32)
            back = lax.dot_general(tile, c_all[r], (((0,), (0,)), ((), ())), preferred_element_type=jnp.float32)
            keep = k < used
            terms.append((r, c, jnp.where(keep, ahead, 0.0), jnp.where(keep, back, 0.0)))
        for r, c, ahead, back in terms:
            place = lax.rem(r, PAIR) * (n_feat // PAIR) + lax.div(r, PAIR)
            p_sum[place] += ahead
            b_sum[c] += back
        return carry

    lax.fori_loop(0, lax.div(used + group - 1, group), step, 0)

    def round_p(r, carry):
        p_out[r] = p_sum[r].astype(jnp.bfloat16)
        return carry

    lax.fori_loop(0, n_feat, round_p, 0)
    total = None
    for c in range(n_nodes):
        b = b_sum[c].astype(jnp.bfloat16)
        b_out[c] = b
        term = lax.dot_general(x_all[c], b, (((0,), (0,)), ((), ())), preferred_element_type=jnp.float32)
        total = term if total is None else total + term
    w_out[...] = total.reshape(w_out.shape)


def sparse(tile_rows, tile_cols, live, tiles, x_all, c_all):
    n_nodes, rows, width = x_all.shape
    n_feat = c_all.shape[0]
    return pl.pallas_call(
        functools.partial(sparse_kernel, 4),
        out_shape=(
            jax.ShapeDtypeStruct((n_feat, rows, width), jnp.bfloat16),
            jax.ShapeDtypeStruct((n_nodes, rows, width), jnp.bfloat16),
            jax.ShapeDtypeStruct((n_nodes, width // n_nodes, width), jnp.float32),
        ),
        in_specs=[SMEM, SMEM, SMEM, VMEM, VMEM, VMEM],
        out_specs=(VMEM, VMEM, VMEM),
        scratch_shapes=[
            pltpu.VMEM((n_feat, rows, width), jnp.float32),
            pltpu.VMEM((n_nodes, rows, width), jnp.float32),
        ],
        compiler_params=pltpu.CompilerParams(vmem_limit_bytes=LIMIT),
        name="sparse_products",
    )(tile_rows, tile_cols, live, tiles, x_all, c_all)


def split_dot(value, weight, dims):
    high = value.astype(jnp.bfloat16)
    low = (value - high.astype(jnp.float32)).astype(jnp.bfloat16)
    return sum(
        lax.dot_general(part, weight, (dims, ((), ())), preferred_element_type=jnp.float32) for part in (high, low)
    )


def wide(value):
    return value.astype(jnp.float32)


def sum_kernel(
    n_nodes, n_feat, scale,
    p_ref, b_ref, w_ref, weight_ref, out_ref, fg_ref, wg_ref,
    c_rx, x_tx, x_rx, z_tx, z_rx, y_rx, l_tx, l_rx, w1, w4, wz, wn,
    cs, cr, xs, xr, zs, zr, ys, yr, ls, lr, w1s, w1r, w4s, w4r, wzs, wzr, wns, wnr,
):
    at = Place(n_nodes, n_feat)
    nz, ny = at.nz, at.ny
    sibling = (at.i, at.feat(at.xh, at.z, 1 - at.core))
    across = (at.i, at.feat(1 - at.xh, at.z, at.core))
    slanted = (at.i, at.feat(1 - at.xh, at.z, 1 - at.core))
    beside = (at.node(at.y, 1 - at.xl), at.j)

    def node_peer(t):
        i = lax.rem(at.i + t, n_nodes)
        return i, (i, at.j)

    def y_peer(t):
        y = lax.rem(at.y + t, ny)
        return y, (at.node(y, at.xl), at.j)

    def z_peer(t):
        k = lax.div(nz - 1 - t, 2) + lax.rem(nz - 1 - t, 2)
        off = lax.rem(t, 2) * (nz - 2 * k) + k
        z = lax.rem(at.z + off, nz)
        return z, (at.i, at.feat(at.xh, z, at.core))

    greet(
        [sibling, across, slanted]
        + [node_peer(t)[1] for t in range(1, n_nodes)]
        + [z_peer(t)[1] for t in range(nz - 1)]
    )

    def loop(start, stop, body):
        lax.fori_loop(start, stop, lambda t, carry: (body(t), carry)[1], 0)

    def w1_copy(t):
        i, device = node_peer(t)
        return remote(w_ref.at[i], w1.at[at.i], w1s.at[i], w1r.at[at.i], device)

    loop(1, n_nodes, lambda t: w1_copy(t).start())

    def c_copy(xh, z):
        slot = xh * nz + z
        return remote(
            p_ref.at[(1 - at.core) * 2 * nz + slot], c_rx.at[slot], cs.at[slot], cr.at[slot], sibling
        )

    def own_p(xh, z):
        return wide(p_ref[(at.core * 2 + xh) * nz + z])

    loop(0, nz - 1, lambda t: c_copy(1 - at.xh, z_peer(t)[0]).start())
    c_copy(1 - at.xh, at.z).start()
    loop(0, nz - 1, lambda t: c_copy(at.xh, z_peer(t)[0]).start())
    c_copy(at.xh, at.z).start()

    def y_copy(t):
        y, device = y_peer(t)
        return remote(b_ref.at[pl.ds(y * PAIR, PAIR)], y_rx.at[at.y], ys.at[y], yr.at[at.y], device)

    loop(1, ny, lambda t: y_copy(t).start())

    def x_copy(z):
        return remote(x_tx.at[z], x_rx.at[z], xs.at[z], xr.at[z], across)

    def x_step(z):
        c_copy(1 - at.xh, z).wait_recv()
        x_tx[z] = (own_p(1 - at.xh, z) + wide(c_rx[(1 - at.xh) * nz + z])).astype(jnp.bfloat16)
        x_copy(z).start()

    loop(0, nz - 1, lambda t: x_step(z_peer(t)[0]))
    x_step(at.z)

    def w1_arrival(t):
        i, device = node_peer(t)
        remote(w_ref.at[at.i], w1.at[i], w1s.at[i], w1r.at[i], device).wait_recv()

    w1[at.i] = w_ref[at.i]
    loop(1, n_nodes, w1_arrival)
    me4 = at.xh * 2 + at.core
    w4[me4] = jnp.sum(w1[...], axis=0)
    four = [
        (at.xh * 2 + 1 - at.core, sibling),
        ((1 - at.xh) * 2 + at.core, across),
        ((1 - at.xh) * 2 + 1 - at.core, slanted),
    ]
    for slot, device in four:
        remote(w4.at[me4], w4.at[me4], w4s.at[slot], w4r.at[me4], device).start()

    def z_copy(t):
        z, device = z_peer(t)
        return remote(z_tx.at[z], z_rx.at[at.z], zs.at[z], zr.at[at.z], device)

    def four_sum(z):
        c_copy(at.xh, z).wait_recv()
        x_copy(z).wait_recv()
        return own_p(at.xh, z) + wide(c_rx[at.xh * nz + z]) + wide(x_rx[z])

    def z_step(t):
        z = z_peer(t)[0]
        z_tx[z] = four_sum(z).astype(jnp.bfloat16)
        z_copy(t).start()

    loop(0, nz - 1, z_step)
    mine = four_sum(at.z)

    for slot, device in four:
        remote(w4.at[slot], w4.at[slot], w4s.at[slot], w4r.at[slot], device).wait_recv()
    wz[at.z] = jnp.sum(w4[...], axis=0)

    def wz_copy(t):
        z, device = z_peer(t)
        return remote(wz.at[at.z], wz.at[at.z], wzs.at[z], wzr.at[at.z], device)

    loop(0, nz - 1, lambda t: wz_copy(t).start())

    def y_arrival(t):
        y, device = y_peer(t)
        remote(b_ref.at[pl.ds(y * PAIR, PAIR)], y_rx.at[y], ys.at[y], yr.at[y], device).wait_recv()

    loop(1, ny, y_arrival)

    def y_sum(xl):
        def add(t, total):
            return total + wide(y_rx[y_peer(t)[0], xl])

        return lax.fori_loop(1, ny, add, wide(b_ref[at.node(at.y, xl)]))

    l_copy = remote(l_tx, l_rx, ls, lr, beside)
    l_tx[...] = y_sum(1 - at.xl).astype(jnp.bfloat16)
    l_copy.start()
    near = y_sum(at.xl)

    def wz_arrival(t):
        z, device = z_peer(t)
        remote(wz.at[z], wz.at[z], wzs.at[z], wzr.at[z], device).wait_recv()

    loop(0, nz - 1, wz_arrival)
    wn[at.i] = jnp.sum(wz[...], axis=0) * scale

    def wn_copy(t):
        i, device = node_peer(t)
        return remote(wn.at[at.i], wn.at[at.i], wns.at[i], wnr.at[at.i], device)

    loop(1, n_nodes, lambda t: wn_copy(t).start())

    l_copy.wait_recv()
    fg_ref[...] = split_dot(near + wide(l_rx[...]), weight_ref[...], ((1,), (1,))).astype(fg_ref.dtype)

    def z_arrival(t, total):
        z, device = z_peer(t)
        remote(z_tx.at[z], z_rx.at[z], zs.at[z], zr.at[z], device).wait_recv()
        return total + wide(z_rx[z])

    whole = lax.fori_loop(0, nz - 1, z_arrival, mine)
    out_ref[...] = split_dot(whole, weight_ref[...], ((1,), (0,))).astype(out_ref.dtype)

    def wn_arrival(t):
        i, device = node_peer(t)
        remote(wn.at[i], wn.at[i], wns.at[i], wnr.at[i], device).wait_recv()

    loop(1, n_nodes, wn_arrival)
    wg_ref[...] = wn[...]

    loop(1, n_nodes, lambda t: w1_copy(t).wait_send())
    for xh in (0, 1):
        loop(0, nz, lambda z: c_copy(xh, z).wait_send())
    loop(1, ny, lambda t: y_copy(t).wait_send())
    loop(0, nz, lambda z: x_copy(z).wait_send())
    for slot, device in four:
        remote(w4.at[me4], w4.at[me4], w4s.at[slot], w4r.at[me4], device).wait_send()
    loop(0, nz - 1, lambda t: z_copy(t).wait_send())
    loop(0, nz - 1, lambda t: wz_copy(t).wait_send())
    l_copy.wait_send()
    loop(1, n_nodes, lambda t: wn_copy(t).wait_send())


def sum_up(n_nodes, n_feat, scale, partial, back, term, weight):
    rows, width = partial.shape[1:]
    ny, nz = n_nodes // PAIR, n_feat // (PAIR * PAIR)
    dma = pltpu.SemaphoreType.DMA
    share = width // n_nodes

    def blocks(*lead):
        return pltpu.VMEM((*lead, rows, width), jnp.bfloat16)

    def shares(count):
        return pltpu.VMEM((count, share, width), jnp.float32)

    counts = (2 * nz, nz, nz, ny, None, n_nodes, 4, nz, n_nodes)
    sems = []
    for count in counts:
        sems += [dma if count is None else dma((count,))] * 2
    return pl.pallas_call(
        functools.partial(sum_kernel, n_nodes, n_feat, scale),
        out_shape=(
            jax.ShapeDtypeStruct((rows, width), jnp.bfloat16),
            jax.ShapeDtypeStruct((rows, width), jnp.bfloat16),
            jax.ShapeDtypeStruct((n_nodes, share, width), jnp.float32),
        ),
        in_specs=[VMEM] * 4,
        out_specs=(VMEM,) * 3,
        scratch_shapes=[
            blocks(2 * nz),
            blocks(nz),
            blocks(nz),
            blocks(nz),
            blocks(nz),
            blocks(ny, PAIR),
            blocks(),
            blocks(),
            shares(n_nodes),
            shares(4),
            shares(nz),
            shares(n_nodes),
        ]
        + sems,
        compiler_params=pltpu.CompilerParams(collective_id=1, has_side_effects=True, vmem_limit_bytes=LIMIT),
        name="sum_blocks",
    )(partial, back, term, weight)


def body(n_nodes, n_feat, features, weight, tiles, tile_rows, tile_cols, live, cotangent):
    scale = 1.0 / math.sqrt(features.shape[0] * n_nodes * n_feat)
    x_all, c_all = gather(n_nodes, n_feat, features, cotangent)
    partial, back, term = sparse(tile_rows, tile_cols, live, tiles, x_all, c_all)
    output, feature_grad, weight_grad = sum_up(n_nodes, n_feat, scale, partial, back, term, weight)
    return output, feature_grad, weight_grad.reshape(weight.shape)


def solution(mesh):
    in_specs = (
        P(("feat", "nodes"), None),
        P(),
        P(("nodes", "feat"), None, None),
        P(("nodes", "feat")),
        P(("nodes", "feat")),
        P(("nodes", "feat")),
        P(("nodes", "feat"), None),
    )
    out_specs = (P(("nodes", "feat"), None), P(("feat", "nodes"), None), P())
    step = functools.partial(body, mesh.shape["nodes"], mesh.shape["feat"])
    return jax.shard_map(step, mesh=mesh, in_specs=in_specs, out_specs=out_specs, check_vma=False)
```

time: 970 us -> 122 us (0.13)
  waiting for transfers between devices: 898 us -> 0 us
  Pallas kernels: 0 us -> 114 us
  matrix products: 32 us -> 0 us
  local copies, waits for them, and re-layouts: 22.2 us -> 6.35 us
  between operations: 14.5 us -> 1.37 us
    psum x1 -> x0, waiting for transfers between devices: 470 us -> none  [body(): lax.psum(local_term, ('nodes', 'feat')) * (1.0 / math.sqrt(nodes_total))]
    reduce_scatter x2 -> x0, waiting for transfers between devices: 256 us -> none  [the longest x1 200 us: body(): lax.psum_scatter(partial_value, 'feat', scatter_dimension=0, tiled=True)]
    all_gather x2 -> x0, waiting for transfers between devices: 171 us -> none  [the longest x1 133 us: body(): cotangent_whole = lax.all_gather(cotangent, 'feat', axis=0, tiled=True)]
    pallas_call x0 -> x3, Pallas kernels: none -> 114 us  [the longest x1 62.5 us: sum_up(): pl.pallas_call(functools.partial(sum_kernel, n_nodes, n_feat, scale), out...]
    dot_general x9 -> x0, matrix products: 32 us -> none  [the longest x2 12.8 us: place_tiles(): jnp.einsum('tk,kaf->taf', place, terms, precision=lax.Precision.HIGHEST)]
    dot_general x4 -> x0, local copies, waits for them, and re-layouts: 22.1 us -> none  [the longest x2 8.84 us: place_tiles(): jnp.einsum('tk,kaf->taf', place, terms, precision=lax.Precision.HIGHEST)]
  transfers between devices with their start and end apart: 5 -> 0, of which waited for: 5 -> 0; matrix products, arithmetic and copies ran while one was open for 6% -> 0% of each run, Pallas kernels for 0% -> 0%
where the time goes in v1:
time: 122 us; the launch traced here: 121 us
  Pallas kernels  114 us (93%)
  local copies, waits for them, and re-layouts  6.35 us (5%)
  between operations  1.37 us (1%)
    pallas_call x1, Pallas kernels, sum_up(): pl.pallas_call(functools.partial(sum_kernel, n_nodes, n_feat, scale), out...  62.5 us
    pallas_call x1, Pallas kernels, gather(): pl.pallas_call(functools.partial(gather_kernel, n_nodes, n_feat), out_sha...  45.6 us
    unnamed x15, local copies, waits for them, and re-layouts  6.35 us
    pallas_call x1, Pallas kernels, sparse(): pl.pallas_call(functools.partial(sparse_kernel, 4), out_shape=(jax.ShapeD...  5.46 us

profile of v1, /device:TPU:1, one launch (start us, length us, event | category | flops | bytes accessed | tf_op | source)
XLA Modules:
  0.0 121.3 jit_solution(7967234373927026945)
XLA Ops:
  0.6 0.0 copy-start.1
  1.3 0.0 copy-start.2
  1.3 0.8 copy-done.2
  2.2 0.0 copy-start.3
  2.2 0.8 copy-done.3
  3.0 45.6 %gather_blocks.1 = (bf16[16,128,256]{2,1,0:T(8,128)(2,1)S(1)}, bf16[48,128,256]{2,1,0:T(8,128)(2,1)S(1)}) custom-call(bf16[128,256]{1,0:T(8,128)(2,1)S(1)} %copy-done.2, bf16[128,256]{1,0:T(8,128)(2,1)S(1)} %copy-done.3), custom_call_target="tpu_custom_call" | custom-call | tf_op jit(solution)/shard_map/gather_blocks/pallas_call | solution.py:160
  48.6 0.0 copy-start
  48.6 1.4 %copy-done = bf16[48,128,128]{2,1,0:T(8,128)(2,1)S(1)} copy-done((bf16[48,128,128]{2,1,0:T(8,128)(2,1)S(1)}, bf16[48,128,128]{2,1,0:T(8,128)(2,1)}, u32[]{:S(2)}) %copy-start) | copy-done | bytes 1572888
  50.0 0.0 copy-start.4
  50.0 0.7 copy-done.4
  50.7 0.0 copy-start.5
  50.7 0.7 copy-done.5
  51.3 5.5 %sparse_products.1 = (bf16[48,128,256]{2,1,0:T(8,128)(2,1)S(1)}, bf16[16,128,256]{2,1,0:T(8,128)(2,1)S(1)}, f32[16,16,256]{2,1,0:T(8,128)S(1)}) custom-call(s32[48]{0:T(128)S(1)} %copy-done.4, s32[48]{0:T(128)S(1)} %copy-done.5, s32[1]{0:T(128)S(6)} %copy.13.live, bf16[48,128,128]{2,1,0:T(8,128)(2,1)S(1)} %copy-done, ...), custom_call_target="tpu_custom_call" | custom-call | tf_op jit(solution)/shard_map/sparse_products/pallas_call | solution.py:236
  56.8 0.0 copy-done.1
  56.8 62.5 %sum_blocks.1 = (bf16[128,256]{1,0:T(8,128)(2,1)S(1)}, bf16[128,256]{1,0:T(8,128)(2,1)S(1)}, f32[16,16,256]{2,1,0:T(8,128)S(1)}) custom-call(bf16[48,128,256]{2,1,0:T(8,128)(2,1)S(1)} %get-tuple-element.13.p_ref, bf16[16,128,256]{2,1,0:T(8,128)(2,1)S(1)} %get-tuple-element.14.b_ref, f32[16,16,256]{2,1,0:T(8,128)S(1)} %get-tuple-element.15.w_ref, ...), custom_call_target="tpu_custom_call" | custom-call | tf_op jit(solution)/shard_map/sum_blocks/pallas_call | solution.py:459
  119.4 0.6 copy.14
  120.0 0.6 copy.15
  120.6 0.7 copy.16
Async XLA Ops:
  0.6 56.2 %copy-start.1 = (bf16[256,256]{1,0:T(8,128)(2,1)S(1)}, bf16[256,256]{1,0:T(8,128)(2,1)}, u32[]{:S(2)}) copy-start(bf16[256,256]{1,0:T(8,128)(2,1)} %weight_ref.1) | copy-start | bytes 393220
  1.3 0.8 copy-start.2
  2.2 0.8 copy-start.3
  48.6 1.4 %copy-start = (bf16[48,128,128]{2,1,0:T(8,128)(2,1)S(1)}, bf16[48,128,128]{2,1,0:T(8,128)(2,1)}, u32[]{:S(2)}) copy-start(bf16[48,128,128]{2,1,0:T(8,128)(2,1)} %tiles.1) | copy-start | bytes 4718596
  50.0 0.7 copy-start.4
  50.7 0.7 copy-start.5

commit v2 on v0

v2 whole, which is shorter than its diff:
```python
import functools
import math

import jax
import jax.numpy as jnp
from jax import lax
from jax.experimental import pallas as pl
from jax.experimental.pallas import tpu as pltpu
from jax.sharding import PartitionSpec as P

MESH = pl.DeviceIdType.MESH
VMEM = pl.BlockSpec(memory_space=pltpu.VMEM)
ANY = pl.BlockSpec(memory_space=pl.ANY)
SMEM = pl.BlockSpec(memory_space=pltpu.SMEM)
LIMIT = 52 * 1024 * 1024
GROUP = 4
PAIR = 2


class Place:
    def __init__(self, n_nodes, n_feat):
        self.n_nodes, self.n_feat = n_nodes, n_feat
        self.ny, self.nz = n_nodes // PAIR, n_feat // (PAIR * PAIR)
        self.i, self.j = lax.axis_index("nodes"), lax.axis_index("feat")
        self.y, self.xl = lax.div(self.i, PAIR), lax.rem(self.i, PAIR)
        self.xh = lax.div(self.j, PAIR * self.nz)
        self.z = lax.rem(lax.div(self.j, PAIR), self.nz)
        self.core = lax.rem(self.j, PAIR)

    def node(self, y, xl):
        return y * PAIR + xl

    def feat(self, xh, z, core):
        return (xh * self.nz + z) * PAIR + core


def greet(partners):
    barrier = pltpu.get_barrier_semaphore()
    for device in partners:
        pl.semaphore_signal(barrier, inc=1, device_id=device, device_id_type=MESH)
    pl.semaphore_wait(barrier, len(partners))


def remote(src, dst, send_sem, recv_sem, device):
    return pltpu.make_async_remote_copy(
        src_ref=src, dst_ref=dst, send_sem=send_sem, recv_sem=recv_sem, device_id=device, device_id_type=MESH
    )


def wide(value):
    return value.astype(jnp.float32)


def split_dot(value, weight, dims):
    high = value.astype(jnp.bfloat16)
    low = (value - wide(high)).astype(jnp.bfloat16)
    return sum(
        lax.dot_general(part, weight, (dims, ((), ())), preferred_element_type=jnp.float32) for part in (high, low)
    )


def chains(tile_rows, tile_cols, live, row_count, col_count):
    slot = jnp.arange(tile_rows.shape[0], dtype=jnp.int32)

    def before(values):
        same = (values[:, None] == values[None, :]) & (slot[None, :] < slot[:, None])
        return jnp.max(jnp.where(same, slot[None, :], -1), axis=1)

    def last(values, count):
        places = jnp.arange(count, dtype=jnp.int32)
        same = (values[None, :] == places[:, None]) & (slot[None, :] < live[0])
        return jnp.max(jnp.where(same, slot[None, :], -1), axis=1)

    return jnp.concatenate(
        [
            tile_rows,
            tile_cols,
            before(tile_rows),
            before(tile_cols),
            last(tile_rows, row_count),
            last(tile_cols, col_count),
        ]
    )


def kernel(
    n_nodes, n_feat, scale,
    index, x_ref, c_ref, weight_ref, tiles_ref, out_ref, fg_ref, wg_ref,
    tiles, x_all, c_all, ahead, back, p_tx, b_tx, c_rx, x_tx, x_rx, z_tx, z_rx, y_rx, l_tx, l_rx,
    w0, w1, w4_tx, w4, wz, w5, wn, tile_sem,
    gxs, gxr, gzs, gzr, gcs, gcr, gls, glr, gys, gyr,
    cs, cr, xs, xr, zs, zr, ys, yr, ls, lr, w1s, w1r, w4s, w4r, wzs, wzr, w5s, w5r, wns, wnr,
):
    at = Place(n_nodes, n_feat)
    nz, ny = at.nz, at.ny
    slots = tiles.shape[0]
    before_row, before_col, last_row, last_col = 2 * slots, 3 * slots, 4 * slots, 4 * slots + n_feat
    z_near = [lax.rem(at.z + 1, nz), lax.rem(at.z + nz - 1, nz)]
    y_near = [lax.rem(at.y + 1, ny), lax.rem(at.y + ny - 1, ny)]
    sibling = (at.i, at.feat(at.xh, at.z, 1 - at.core))
    across = (at.i, at.feat(1 - at.xh, at.z, at.core))
    slanted = (at.i, at.feat(1 - at.xh, at.z, 1 - at.core))
    beside = (at.node(at.y, 1 - at.xl), at.j)
    along_z = [(at.i, at.feat(at.xh, z, at.core)) for z in z_near]
    along_y = [(at.node(y, at.xl), at.j) for y in y_near]

    def node_peer(t):
        i = lax.rem(at.i + t, n_nodes)
        return i, (i, at.j)

    def y_peer(t):
        y = lax.rem(at.y + t, ny)
        return y, (at.node(y, at.xl), at.j)

    def z_peer(t):
        k = lax.div(nz - 1 - t, 2) + lax.rem(nz - 1 - t, 2)
        off = lax.rem(t, 2) * (nz - 2 * k) + k
        z = lax.rem(at.z + off, nz)
        return z, (at.i, at.feat(at.xh, z, at.core))

    def loop(start, stop, body):
        lax.fori_loop(start, stop, lambda t, carry: (body(t), carry)[1], 0)

    tile_copy = pltpu.make_async_copy(tiles_ref, tiles, tile_sem)
    tile_copy.start()
    greet(
        [sibling, across, slanted]
        + [node_peer(t)[1] for t in range(1, n_nodes)]
        + [z_peer(t)[1] for t in range(nz - 1)]
    )

    half_z, half_y = nz // 2, ny // 2

    def last_z(s, d):
        return half_z if s == d else nz - 1 - half_z

    def last_y(s, d):
        return half_y if s == d else ny - 1 - half_y

    def origin(place, count, d, t):
        return lax.rem(place + (count - t if d == 0 else t), count)

    def xh_of(s):
        return at.xh if s == 0 else 1 - at.xh

    def xl_of(s):
        return at.xl if s == 0 else 1 - at.xl

    def gz_copy(s, d, t, origin_z):
        block = c_all.at[at.feat(xh_of(s), origin_z, at.core)]
        src = c_ref if (s == 0 and t == 1) else block
        return remote(src, block, gzs.at[s, d, t - 1], gzr.at[s, d, t - 1], along_z[d])

    def sibling_copy(s, origin_z, src=None, arriving=False):
        core = 1 - at.core if arriving else at.core
        block = c_all.at[at.feat(xh_of(s), origin_z, core)]
        k = s * nz + origin_z
        return remote(block if src is None else src, block, gcs.at[k], gcr.at[k], sibling)

    def gy_copy(s, d, t, origin_y):
        block = x_all.at[at.node(origin_y, xl_of(s))]
        src = x_ref if (s == 0 and t == 1) else block
        return remote(src, block, gys.at[s, d, t - 1], gyr.at[s, d, t - 1], along_y[d])

    z_sent, y_sent = [], []

    def z_start(s, d, t):
        copy = gz_copy(s, d, t, origin(at.z, nz, d, t - 1))
        copy.start()
        z_sent.append(copy)

    def y_start(s, d, t):
        copy = gy_copy(s, d, t, origin(at.y, ny, d, t - 1))
        copy.start()
        y_sent.append(copy)

    def across_copy(xh):
        return remote(c_ref, c_all.at[at.feat(xh, at.z, at.core)], gxs, gxr, across)

    def beside_copy(xl):
        return remote(x_ref, x_all.at[at.node(at.y, xl)], gls, glr, beside)

    across_copy(at.xh).start()
    beside_copy(at.xl).start()
    for d in (0, 1):
        z_start(0, d, 1)
        y_start(0, d, 1)
    sent_over = [sibling_copy(0, at.z, c_ref)]
    sent_over[0].start()
    c_all[at.j] = c_ref[...]
    x_all[at.i] = x_ref[...]
    beside_copy(1 - at.xl).wait_recv()
    for d in (0, 1):
        y_start(1, d, 1)
    across_copy(1 - at.xh).wait_recv()
    for d in (0, 1):
        z_start(1, d, 1)
    copy = sibling_copy(1, at.z)
    copy.start()
    sent_over.append(copy)


    def y_arrive(t):
        for s in (0, 1):
            for d in (0, 1):
                if t <= last_y(s, d):
                    gy_copy(s, d, t, origin(at.y, ny, d, t)).wait_recv()
                    if t < last_y(s, d):
                        y_start(s, d, t + 1)

    def z_arrive(s, d, t):
        if t <= last_z(s, d):
            origin_z = origin(at.z, nz, d, t)
            gz_copy(s, d, t, origin_z).wait_recv()
            if t < last_z(s, d):
                z_start(s, d, t + 1)
            over = sibling_copy(s, origin_z)
            over.start()
            sent_over.append(over)

    ways = [(s, d) for s in (0, 1) for d in (0, 1)]
    split = max(1, half_z - 2)
    for t in range(1, max(split, half_y) + 1):
        if t <= half_y:
            y_arrive(t)
        if t <= split:
            for s, d in ways:
                z_arrive(s, d, t)

    def add_chain(sums, terms, before, k0):
        for u, term in enumerate(terms):
            prev = index[before + k0 + u]
            sums[k0 + u] = term + jnp.where(prev >= 0, sums[jnp.maximum(prev, 0)], 0.0)

    def ahead_step(g):
        terms = [
            jnp.dot(tiles[g * GROUP + u], x_all[index[slots + g * GROUP + u]], preferred_element_type=jnp.float32)
            for u in range(GROUP)
        ]
        add_chain(ahead, terms, before_row, g * GROUP)

    def back_step(g):
        terms = [
            lax.dot_general(
                tiles[g * GROUP + u], c_all[index[g * GROUP + u]], (((0,), (0,)), ((), ())),
                preferred_element_type=jnp.float32,
            )
            for u in range(GROUP)
        ]
        add_chain(back, terms, before_col, g * GROUP)

    def own_p(xh, z, core):
        k = index[last_row + at.feat(xh, z, core)]
        return jnp.where(k >= 0, ahead[jnp.maximum(k, 0)], 0.0)

    def own_b(y, xl):
        k = index[last_col + at.node(y, xl)]
        return jnp.where(k >= 0, back[jnp.maximum(k, 0)], 0.0)

    groups = slots // GROUP
    tile_copy.wait()
    done = 0
    rest = [(s, d, t) for t in range(split + 1, half_z) for s, d in ways]
    for n, (s, d, t) in enumerate(rest):
        z_arrive(s, d, t)
        upto = groups * (n + 1) // len(rest)
        loop(done, upto, ahead_step)
        done = upto
    loop(done, groups, ahead_step)

    def c_copy(xh, z):
        slot = xh * nz + z
        return remote(p_tx.at[slot], c_rx.at[slot], cs.at[slot], cr.at[slot], sibling)

    def c_step(xh, z):
        p_tx[xh * nz + z] = own_p(xh, z, 1 - at.core).astype(jnp.bfloat16)
        c_copy(xh, z).start()

    loop(0, nz - 1, lambda t: c_step(1 - at.xh, z_peer(t)[0]))
    c_step(1 - at.xh, at.z)
    for s, d in ways:
        z_arrive(s, d, half_z)
    loop(0, nz - 1, lambda t: c_step(at.xh, z_peer(t)[0]))
    c_step(at.xh, at.z)

    def x_copy(z):
        return remote(x_tx.at[z], x_rx.at[z], xs.at[z], xr.at[z], across)

    def x_step(z):
        c_copy(1 - at.xh, z).wait_recv()
        x_tx[z] = (own_p(1 - at.xh, z, at.core) + wide(c_rx[(1 - at.xh) * nz + z])).astype(jnp.bfloat16)
        x_copy(z).start()

    loop(0, nz - 1, lambda t: x_step(z_peer(t)[0]))
    x_step(at.z)

    for s in (0, 1):
        for z in range(nz):
            sibling_copy(s, z, arriving=True).wait_recv()
    loop(0, groups, back_step)
    total = None
    for i in range(n_nodes):
        b_tx[i] = own_b(i // PAIR, i % PAIR).astype(jnp.bfloat16)
        term = lax.dot_general(x_all[i], b_tx[i], (((0,), (0,)), ((), ())), preferred_element_type=jnp.float32)
        total = term if total is None else total + term
    w0[...] = total.astype(w0.dtype).reshape(w0.shape)

    def w1_copy(t):
        i, device = node_peer(t)
        return remote(w0.at[i], w1.at[at.i], w1s.at[i], w1r.at[at.i], device)

    loop(1, n_nodes, lambda t: w1_copy(t).start())

    def y_copy(t):
        y, device = y_peer(t)
        return remote(b_tx.at[pl.ds(y * PAIR, PAIR)], y_rx.at[at.y], ys.at[y], yr.at[at.y], device)

    loop(1, ny, lambda t: y_copy(t).start())

    def z_copy(t):
        z, device = z_peer(t)
        return remote(z_tx.at[z], z_rx.at[at.z], zs.at[z], zr.at[at.z], device)

    def four_sum(z):
        c_copy(at.xh, z).wait_recv()
        x_copy(z).wait_recv()
        return own_p(at.xh, z, at.core) + wide(c_rx[at.xh * nz + z]) + wide(x_rx[z])

    def z_step(t):
        z = z_peer(t)[0]
        z_tx[z] = four_sum(z).astype(jnp.bfloat16)
        z_copy(t).start()

    first, second = nz // 3, 2 * nz // 3
    loop(0, first, z_step)

    def w1_arrival(t):
        i, device = node_peer(t)
        remote(w0.at[i], w1.at[i], w1s.at[i], w1r.at[i], device).wait_recv()

    w1[at.i] = w0[at.i]
    loop(1, n_nodes, w1_arrival)
    me4 = at.xh * 2 + at.core
    shared = jnp.sum(wide(w1[...]), axis=0)
    for slot in range(4):
        row, column = slot // 2 * 8, slot % 2 * 128
        w4_tx[slot] = shared[row : row + 8, column : column + 128]
    w4[me4] = w4_tx[me4]
    four = [
        (at.xh * 2 + 1 - at.core, sibling),
        ((1 - at.xh) * 2 + at.core, across),
        ((1 - at.xh) * 2 + 1 - at.core, slanted),
    ]

    def w4_copy(slot, device):
        return remote(w4_tx.at[slot], w4.at[me4], w4s.at[slot], w4r.at[me4], device)

    for slot, device in four:
        w4_copy(slot, device).start()
    loop(first, second, z_step)

    for slot, device in four:
        remote(w4_tx.at[slot], w4.at[slot], w4s.at[slot], w4r.at[slot], device).wait_recv()
    wz[at.z] = jnp.sum(w4[...], axis=0)

    def wz_copy(t):
        z, device = z_peer(t)
        return remote(wz.at[at.z], wz.at[at.z], wzs.at[z], wzr.at[at.z], device)

    loop(0, nz - 1, lambda t: wz_copy(t).start())
    loop(second, nz - 1, z_step)
    mine = four_sum(at.z)

    def wz_arrival(t):
        z, device = z_peer(t)
        remote(wz.at[z], wz.at[z], wzs.at[z], wzr.at[z], device).wait_recv()

    loop(0, nz - 1, wz_arrival)
    w5[me4] = jnp.sum(wz[...], axis=0) * scale

    def w5_copy(slot, device):
        return remote(w5.at[me4], w5.at[me4], w5s.at[slot], w5r.at[me4], device)

    for slot, device in four:
        w5_copy(slot, device).start()
    for slot, device in four:
        remote(w5.at[slot], w5.at[slot], w5s.at[slot], w5r.at[slot], device).wait_recv()
    wn[at.i] = jnp.concatenate(
        [jnp.concatenate([w5[2 * half], w5[2 * half + 1]], axis=1) for half in (0, 1)], axis=0
    ).astype(wn.dtype)

    def wn_copy(t):
        i, device = node_peer(t)
        return remote(wn.at[at.i], wn.at[at.i], wns.at[i], wnr.at[at.i], device)

    loop(1, n_nodes, lambda t: wn_copy(t).start())

    def y_arrival(t):
        y, device = y_peer(t)
        remote(b_tx.at[pl.ds(y * PAIR, PAIR)], y_rx.at[y], ys.at[y], yr.at[y], device).wait_recv()

    loop(1, ny, y_arrival)

    def y_sum(xl):
        def add(t, total):
            return total + wide(y_rx[y_peer(t)[0], xl])

        return lax.fori_loop(1, ny, add, own_b(at.y, xl))

    l_copy = remote(l_tx, l_rx, ls, lr, beside)
    l_tx[...] = y_sum(1 - at.xl).astype(jnp.bfloat16)
    l_copy.start()
    near = y_sum(at.xl)

    def z_arrival(t, total):
        z, device = z_peer(t)
        remote(z_tx.at[z], z_rx.at[z], zs.at[z], zr.at[z], device).wait_recv()
        return total + wide(z_rx[z])

    whole = lax.fori_loop(0, nz - 1, z_arrival, mine)
    out_ref[...] = split_dot(whole, weight_ref[...], ((1,), (0,))).astype(out_ref.dtype)

    l_copy.wait_recv()
    fg_ref[...] = split_dot(near + wide(l_rx[...]), weight_ref[...], ((1,), (1,))).astype(fg_ref.dtype)

    def wn_arrival(t):
        i, device = node_peer(t)
        remote(wn.at[i], wn.at[i], wns.at[i], wnr.at[i], device).wait_recv()

    loop(1, n_nodes, wn_arrival)
    wg_ref[...] = wide(wn[...])

    for sent in sent_over + z_sent + y_sent:
        sent.wait_send()
    across_copy(at.xh).wait_send()
    beside_copy(at.xl).wait_send()
    for xh in (0, 1):
        loop(0, nz, lambda z: c_copy(xh, z).wait_send())
    loop(0, nz, lambda z: x_copy(z).wait_send())
    loop(1, n_nodes, lambda t: w1_copy(t).wait_send())
    loop(1, ny, lambda t: y_copy(t).wait_send())
    loop(0, nz - 1, lambda t: z_copy(t).wait_send())
    for slot, device in four:
        w4_copy(slot, device).wait_send()
        w5_copy(slot, device).wait_send()
    loop(0, nz - 1, lambda t: wz_copy(t).wait_send())
    l_copy.wait_send()
    loop(1, n_nodes, lambda t: wn_copy(t).wait_send())


def body(n_nodes, n_feat, features, weight, tiles, tile_rows, tile_cols, live, cotangent):
    rows, width = features.shape
    scale = 1.0 / math.sqrt(rows * n_nodes * n_feat)
    ny, nz = n_nodes // PAIR, n_feat // (PAIR * PAIR)
    slots, side = tiles.shape[:2]
    share = width // n_nodes
    dma = pltpu.SemaphoreType.DMA

    def blocks(*lead, kind=jnp.bfloat16):
        return pltpu.VMEM((*lead, rows, width), kind)

    def shares(count, kind):
        return pltpu.VMEM((count, share, width), kind)

    def pieces(count):
        return pltpu.VMEM((count, share // 2, width // 2), jnp.float32)

    def pairs(*counts):
        return [sem for count in counts for sem in [dma(count) if count else dma] * 2]

    index = chains(tile_rows, tile_cols, live, n_feat, n_nodes)
    output, feature_grad, weight_grad = pl.pallas_call(
        functools.partial(kernel, n_nodes, n_feat, scale),
        out_shape=(
            jax.ShapeDtypeStruct((rows, width), jnp.bfloat16),
            jax.ShapeDtypeStruct((rows, width), jnp.bfloat16),
            jax.ShapeDtypeStruct((n_nodes, share, width), jnp.float32),
        ),
        in_specs=[SMEM, VMEM, VMEM, VMEM, ANY],
        out_specs=(VMEM,) * 3,
        scratch_shapes=[
            pltpu.VMEM(tiles.shape, tiles.dtype),
            blocks(n_nodes),
            blocks(n_feat),
            blocks(slots, kind=jnp.float32),
            blocks(slots, kind=jnp.float32),
            blocks(2 * nz),
            blocks(n_nodes),
            blocks(2 * nz),
            blocks(nz),
            blocks(nz),
            blocks(nz),
            blocks(nz),
            blocks(ny, PAIR),
            blocks(),
            blocks(),
            shares(n_nodes, jnp.bfloat16),
            shares(n_nodes, jnp.bfloat16),
            pieces(4),
            pieces(4),
            pieces(nz),
            pieces(4),
            shares(n_nodes, jnp.bfloat16),
            dma,
        ]
        + pairs(None, (2, 2, nz // 2), (2 * nz,), None, (2, 2, ny // 2))
        + pairs((2 * nz,), (nz,), (nz,), (ny,), None)
        + pairs((n_nodes,), (4,), (nz,), (4,), (n_nodes,)),
        compiler_params=pltpu.CompilerParams(collective_id=0, has_side_effects=True, vmem_limit_bytes=LIMIT),
        name="graph_layer",
    )(index, features, cotangent, weight, tiles)
    return output, feature_grad, weight_grad.reshape(weight.shape)


def solution(mesh):
    in_specs = (
        P(("feat", "nodes"), None),
        P(),
        P(("nodes", "feat"), None, None),
        P(("nodes", "feat")),
        P(("nodes", "feat")),
        P(("nodes", "feat")),
        P(("nodes", "feat"), None),
    )
    out_specs = (P(("nodes", "feat"), None), P(("feat", "nodes"), None), P())
    step = functools.partial(body, mesh.shape["nodes"], mesh.shape["feat"])
    return jax.shard_map(step, mesh=mesh, in_specs=in_specs, out_specs=out_specs, check_vma=False)
```

time: 970 us -> 107 us (0.11)
  waiting for transfers between devices: 898 us -> 0 us
  Pallas kernels: 0 us -> 98.7 us
  matrix products: 32 us -> 0 us
  local copies, waits for them, and re-layouts: 22.2 us -> 5.3 us
  between operations: 14.5 us -> 1.3 us
    psum x1 -> x0, waiting for transfers between devices: 470 us -> none  [body(): lax.psum(local_term, ('nodes', 'feat')) * (1.0 / math.sqrt(nodes_total))]
    reduce_scatter x2 -> x0, waiting for transfers between devices: 256 us -> none  [the longest x1 200 us: body(): lax.psum_scatter(partial_value, 'feat', scatter_dimension=0, tiled=True)]
    all_gather x2 -> x0, waiting for transfers between devices: 171 us -> none  [the longest x1 133 us: body(): cotangent_whole = lax.all_gather(cotangent, 'feat', axis=0, tiled=True)]
    pallas_call x0 -> x1, Pallas kernels: none -> 98.7 us  [body(): pl.pallas_call(functools.partial(kernel, n_nodes, n_feat, scale), out_sha...]
    dot_general x9 -> x0, matrix products: 32 us -> none  [the longest x2 12.8 us: place_tiles(): jnp.einsum('tk,kaf->taf', place, terms, precision=lax.Precision.HIGHEST)]
    dot_general x4 -> x0, local copies, waits for them, and re-layouts: 22.1 us -> none  [the longest x2 8.84 us: place_tiles(): jnp.einsum('tk,kaf->taf', place, terms, precision=lax.Precision.HIGHEST)]
  transfers between devices with their start and end apart: 5 -> 0, of which waited for: 5 -> 0; matrix products, arithmetic and copies ran while one was open for 6% -> 0% of each run, Pallas kernels for 0% -> 0%
where the time goes in v2:
time: 107 us
  Pallas kernels  98.7 us (92%)
  local copies, waits for them, and re-layouts  5.3 us (5%)
  other arithmetic  1.75 us (2%)
  between operations  1.3 us (1%)
    pallas_call x1, Pallas kernels, body(): pl.pallas_call(functools.partial(kernel, n_nodes, n_feat, scale), out_sha...  98.7 us
    unnamed x9, local copies, waits for them, and re-layouts  4.55 us

profile of v2, /device:TPU:1, one launch (start us, length us, event | category | flops | bytes accessed | tf_op | source)
XLA Modules:
  0.0 107.1 jit_solution(11003631639634264322)
XLA Ops:
  1.3 0.8 select_reduce_fusion.3
  2.1 1.0 select_reduce_fusion
  3.0 0.8 concatenate.3.index
  3.8 0.0 copy-start
  3.8 0.9 copy-done
  4.7 0.0 copy-start.1
  4.7 0.8 copy-done.1
  5.5 0.0 copy-start.2
  5.5 0.8 copy-done.2
  6.4 98.7 %graph_layer.1 = (bf16[128,256]{1,0:T(8,128)(2,1)S(1)}, bf16[128,256]{1,0:T(8,128)(2,1)S(1)}, f32[16,16,256]{2,1,0:T(8,128)S(1)}) custom-call(s32[256]{0:T(256)S(1)} %concatenate.3.index, bf16[128,256]{1,0:T(8,128)(2,1)S(1)} %copy-done.1, bf16[128,256]{1,0:T(8,128)(2,1)S(1)} %copy-done.2, bf16[256,256]{1,0:T(8,128)(2,1)S(1)} %copy-done, ...), custom_call_target="tpu_custom_call" | custom-call | tf_op jit(solution)/shard_map/graph_layer/pallas_call | solution.py:472
  105.1 0.6 copy.14
  105.8 0.6 copy.15
  106.4 0.7 copy.16
  (1 shorter events, 0.0 us)
Async XLA Ops:
  3.8 0.9 copy-start
  4.7 0.8 copy-start.1
  5.5 0.8 copy-start.2

commit v3 on v2

--- a/solution.py
+++ b/solution.py
@@ -11,8 +11,8 @@
 MESH = pl.DeviceIdType.MESH
 VMEM = pl.BlockSpec(memory_space=pltpu.VMEM)
 ANY = pl.BlockSpec(memory_space=pl.ANY)
-SMEM = pl.BlockSpec(memory_space=pltpu.SMEM)
-LIMIT = 52 * 1024 * 1024
+LIMIT = 60 * 1024 * 1024
+LANES = 128
 GROUP = 4
 PAIR = 2
 
@@ -59,42 +59,44 @@
     )
 
 
-def chains(tile_rows, tile_cols, live, row_count, col_count):
-    slot = jnp.arange(tile_rows.shape[0], dtype=jnp.int32)
-
-    def before(values):
-        same = (values[:, None] == values[None, :]) & (slot[None, :] < slot[:, None])
-        return jnp.max(jnp.where(same, slot[None, :], -1), axis=1)
-
-    def last(values, count):
-        places = jnp.arange(count, dtype=jnp.int32)
-        same = (values[None, :] == places[:, None]) & (slot[None, :] < live[0])
-        return jnp.max(jnp.where(same, slot[None, :], -1), axis=1)
-
-    return jnp.concatenate(
-        [
-            tile_rows,
-            tile_cols,
-            before(tile_rows),
-            before(tile_cols),
-            last(tile_rows, row_count),
-            last(tile_cols, col_count),
-        ]
+def spread_chains(rows, cols, live, row_count, col_count, row_mat, col_mat, chain):
+    slots = rows.shape[0]
+
+    def fill(k, carry):
+        row_mat[pl.ds(k, 1), :] = jnp.full((1, LANES), rows[k], jnp.int32)
+        col_mat[pl.ds(k, 1), :] = jnp.full((1, LANES), cols[k], jnp.int32)
+        return carry
+
+    row_mat[...] = jnp.full(row_mat.shape, -1, jnp.int32)
+    col_mat[...] = jnp.full(col_mat.shape, -1, jnp.int32)
+    lax.fori_loop(0, slots, fill, 0)
+    line = lax.broadcasted_iota(jnp.int32, (LANES, LANES), 0)
+    slot = lax.broadcasted_iota(jnp.int32, (LANES, LANES), 1)
+
+    def best(keep):
+        return jnp.max(jnp.where(keep, slot, -1), axis=1, keepdims=True)
+
+    found = []
+    for mat in (row_mat, col_mat):
+        along, across = mat[...], mat[...].T
+        found.append((best((along == across) & (slot < line)), best((across == line) & (slot < live))))
+    (before_row, last_row), (before_col, last_col) = found
+    chain[...] = jnp.where(
+        slot == 0, before_row, jnp.where(slot == 1, before_col, jnp.where(slot == 2, last_row, last_col))
     )
 
 
 def kernel(
     n_nodes, n_feat, scale,
-    index, x_ref, c_ref, weight_ref, tiles_ref, out_ref, fg_ref, wg_ref,
-    tiles, x_all, c_all, ahead, back, p_tx, b_tx, c_rx, x_tx, x_rx, z_tx, z_rx, y_rx, l_tx, l_rx,
-    w0, w1, w4_tx, w4, wz, w5, wn, tile_sem,
+    rows_ref, cols_ref, live_ref, x_ref, c_ref, weight_in, tiles_ref, out_ref, fg_ref, wg_ref,
+    rows, cols, live, row_mat, col_mat, chain, index, weight_ref, tiles, x_all, c_all, ahead, back, p_tx, b_tx, c_rx, x_tx, x_rx, z_tx, z_rx, y_rx, l_tx, l_rx,
+    w0, w1, w4_tx, w4, wz, w5, wn, load_sem, tile_sem,
     gxs, gxr, gzs, gzr, gcs, gcr, gls, glr, gys, gyr,
     cs, cr, xs, xr, zs, zr, ys, yr, ls, lr, w1s, w1r, w4s, w4r, wzs, wzr, w5s, w5r, wns, wnr,
 ):
     at = Place(n_nodes, n_feat)
     nz, ny = at.nz, at.ny
     slots = tiles.shape[0]
-    before_row, before_col, last_row, last_col = 2 * slots, 3 * slots, 4 * slots, 4 * slots + n_feat
     z_near = [lax.rem(at.z + 1, nz), lax.rem(at.z + nz - 1, nz)]
     y_near = [lax.rem(at.y + 1, ny), lax.rem(at.y + ny - 1, ny)]
     sibling = (at.i, at.feat(at.xh, at.z, 1 - at.core))
@@ -122,12 +124,23 @@
         lax.fori_loop(start, stop, lambda t, carry: (body(t), carry)[1], 0)
 
     tile_copy = pltpu.make_async_copy(tiles_ref, tiles, tile_sem)
+    loads = [
+        pltpu.make_async_copy(src, dst, load_sem.at[k])
+        for k, (src, dst) in enumerate(
+            [
+                (rows_ref, rows),
+                (cols_ref, cols),
+                (live_ref, live),
+                (weight_in, weight_ref),
+                (x_ref, x_all.at[at.i]),
+                (c_ref, c_all.at[at.j]),
+            ]
+        )
+    ]
+    for load in loads:
+        load.start()
     tile_copy.start()
-    greet(
-        [sibling, across, slanted]
-        + [node_peer(t)[1] for t in range(1, n_nodes)]
-        + [z_peer(t)[1] for t in range(nz - 1)]
-    )
+    greet([sibling, across, beside] + along_z + along_y)
 
     half_z, half_y = nz // 2, ny // 2
 
@@ -187,8 +200,11 @@
         y_start(0, d, 1)
     sent_over = [sibling_copy(0, at.z, c_ref)]
     sent_over[0].start()
-    c_all[at.j] = c_ref[...]
-    x_all[at.i] = x_ref[...]
+    for load in loads:
+        load.wait()
+    spread_chains(rows, cols, live[0], n_feat, n_nodes, row_mat, col_mat, chain)
+    chain_copy = pltpu.make_async_copy(chain.at[pl.ds(0, slots)], index, load_sem.at[0])
+    chain_copy.start()
     beside_copy(1 - at.xl).wait_recv()
     for d in (0, 1):
         y_start(1, d, 1)
@@ -229,36 +245,37 @@
 
     def add_chain(sums, terms, before, k0):
         for u, term in enumerate(terms):
-            prev = index[before + k0 + u]
+            prev = index[k0 + u, before]
             sums[k0 + u] = term + jnp.where(prev >= 0, sums[jnp.maximum(prev, 0)], 0.0)
 
     def ahead_step(g):
         terms = [
-            jnp.dot(tiles[g * GROUP + u], x_all[index[slots + g * GROUP + u]], preferred_element_type=jnp.float32)
+            jnp.dot(tiles[g * GROUP + u], x_all[cols[g * GROUP + u]], preferred_element_type=jnp.float32)
             for u in range(GROUP)
         ]
-        add_chain(ahead, terms, before_row, g * GROUP)
+        add_chain(ahead, terms, 0, g * GROUP)
 
     def back_step(g):
         terms = [
             lax.dot_general(
-                tiles[g * GROUP + u], c_all[index[g * GROUP + u]], (((0,), (0,)), ((), ())),
+                tiles[g * GROUP + u], c_all[rows[g * GROUP + u]], (((0,), (0,)), ((), ())),
                 preferred_element_type=jnp.float32,
             )
             for u in range(GROUP)
         ]
-        add_chain(back, terms, before_col, g * GROUP)
+        add_chain(back, terms, 1, g * GROUP)
 
     def own_p(xh, z, core):
-        k = index[last_row + at.feat(xh, z, core)]
+        k = index[at.feat(xh, z, core), 2]
         return jnp.where(k >= 0, ahead[jnp.maximum(k, 0)], 0.0)
 
     def own_b(y, xl):
-        k = index[last_col + at.node(y, xl)]
+        k = index[at.node(y, xl), 3]
         return jnp.where(k >= 0, back[jnp.maximum(k, 0)], 0.0)
 
     groups = slots // GROUP
     tile_copy.wait()
+    chain_copy.wait()
     done = 0
     rest = [(s, d, t) for t in range(split + 1, half_z) for s, d in ways]
     for n, (s, d, t) in enumerate(rest):
@@ -468,7 +485,6 @@
     def pairs(*counts):
         return [sem for count in counts for sem in [dma(count) if count else dma] * 2]
 
-    index = chains(tile_rows, tile_cols, live, n_feat, n_nodes)
     output, feature_grad, weight_grad = pl.pallas_call(
         functools.partial(kernel, n_nodes, n_feat, scale),
         out_shape=(
@@ -476,9 +492,17 @@
             jax.ShapeDtypeStruct((rows, width), jnp.bfloat16),
             jax.ShapeDtypeStruct((n_nodes, share, width), jnp.float32),
         ),
-        in_specs=[SMEM, VMEM, VMEM, VMEM, ANY],
+        in_specs=[ANY] * 7,
         out_specs=(VMEM,) * 3,
         scratch_shapes=[
+            pltpu.SMEM(tile_rows.shape, jnp.int32),
+            pltpu.SMEM(tile_cols.shape, jnp.int32),
+            pltpu.SMEM(live.shape, jnp.int32),
+            pltpu.VMEM((LANES, LANES), jnp.int32),
+            pltpu.VMEM((LANES, LANES), jnp.int32),
+            pltpu.VMEM((LANES, LANES), jnp.int32),
+            pltpu.SMEM((slots, LANES), jnp.int32),
+            pltpu.VMEM(weight.shape, weight.dtype),
             pltpu.VMEM(tiles.shape, tiles.dtype),
             blocks(n_nodes),
             blocks(n_feat),
@@ -501,6 +525,7 @@
             pieces(nz),
             pieces(4),
             shares(n_nodes, jnp.bfloat16),
+            dma((6,)),
             dma,
         ]
         + pairs(None, (2, 2, nz // 2), (2 * nz,), None, (2, 2, ny // 2))
@@ -508,7 +533,7 @@
         + pairs((n_nodes,), (4,), (nz,), (4,), (n_nodes,)),
         compiler_params=pltpu.CompilerParams(collective_id=0, has_side_effects=True, vmem_limit_bytes=LIMIT),
         name="graph_layer",
-    )(index, features, cotangent, weight, tiles)
+    )(tile_rows, tile_cols, live, features, cotangent, weight, tiles)
     return output, feature_grad, weight_grad.reshape(weight.shape)
 
 

time: 107 us -> 102 us (0.953)
  Pallas kernels: 98.7 us -> 95.5 us
  other arithmetic: 1.75 us -> 0 us
    pallas_call x1, Pallas kernels: 98.7 us -> 95.5 us  [body(): pl.pallas_call(functools.partial(kernel, n_nodes, n_feat, scale), out_sha...]
    reduce_max x2 -> x0, other arithmetic: 1.74 us -> none  [last(): return jnp.max(jnp.where(same, slot[None, :], -1), axis=1)]
    unnamed x9 -> x3, local copies, waits for them, and re-layouts: 4.55 us -> 4.61 us
where the time goes in v3:
time: 102 us; the launch traced here: 101 us
  Pallas kernels  95.5 us (94%)
  local copies, waits for them, and re-layouts  4.61 us (5%)
  between operations  1.29 us (1%)
    pallas_call x1, Pallas kernels, body(): pl.pallas_call(functools.partial(kernel, n_nodes, n_feat, scale), out_sha...  95.5 us
    unnamed x3, local copies, waits for them, and re-layouts  4.61 us

profile of v3, /device:TPU:1, one launch (start us, length us, event | category | flops | bytes accessed | tf_op | source)
XLA Modules:
  0.0 101.4 jit_solution(4823896126620585356)
XLA Ops:
  1.3 95.5 %graph_layer.1 = (bf16[128,256]{1,0:T(8,128)(2,1)}, bf16[128,256]{1,0:T(8,128)(2,1)}, f32[16,16,256]{2,1,0:T(8,128)}) custom-call(s32[48]{0:T(128)} %rows_ref.1, s32[48]{0:T(128)} %cols_ref.1, s32[1]{0:T(128)S(6)} %copy.13.live_ref, bf16[128,256]{1,0:T(8,128)(2,1)} %x_ref.1, bf16[128,256]{1,0:T(8,128)(2,1)} %c_ref.1, bf16[256,256]{1,0:T(8,128)(2,1)} %weight_in.1, ...), custom_call_target="tpu_custom_call" | custom-call | tf_op jit(solution)/shard_map/graph_layer/pallas_call | solution.py:488
  96.8 1.5 %copy.14 = bf16[128,256]{1,0:T(8,128)(2,1)} copy(bf16[128,256]{1,0:T(8,128)(2,1)} %get-tuple-element.12) | data formatting | bytes 131072
  98.3 1.5 %copy.15 = bf16[128,256]{1,0:T(8,128)(2,1)} copy(bf16[128,256]{1,0:T(8,128)(2,1)} %get-tuple-element.13) | data formatting | bytes 131072
  99.8 1.7 %copy.16 = f32[256,256]{1,0:T(8,128)} copy(f32[256,256]{1,0:T(8,128)} %bitcast.1) | data formatting | bytes 524288

commit v4 on v3

--- a/solution.py
+++ b/solution.py
@@ -89,10 +89,10 @@
 def kernel(
     n_nodes, n_feat, scale,
     rows_ref, cols_ref, live_ref, x_ref, c_ref, weight_in, tiles_ref, out_ref, fg_ref, wg_ref,
-    rows, cols, live, row_mat, col_mat, chain, index, weight_ref, tiles, x_all, c_all, ahead, back, p_tx, b_tx, c_rx, x_tx, x_rx, z_tx, z_rx, y_rx, l_tx, l_rx,
-    w0, w1, w4_tx, w4, wz, w5, wn, load_sem, tile_sem,
+    rows, cols, live, row_mat, col_mat, chain, index, weight_ref, tiles, x_all, c_all, ahead, back, p_tx, c_rx, x_tx, x_rx, rz_tx, rz_rx, rz_tx32, rz_rx32, ry_tx, ry_rx, l_tx, l_rx,
+    b_all, w0, w1, w4, wz, wn, load_sem, tile_sem,
     gxs, gxr, gzs, gzr, gcs, gcr, gls, glr, gys, gyr,
-    cs, cr, xs, xr, zs, zr, ys, yr, ls, lr, w1s, w1r, w4s, w4r, wzs, wzr, w5s, w5r, wns, wnr,
+    cs, cr, xs, xr, rzs, rzr, rys, ryr, ls, lr, w1s, w1r, w4s, w4r, wzs, wzr, wns, wnr,
 ):
     at = Place(n_nodes, n_feat)
     nz, ny = at.nz, at.ny
@@ -109,10 +109,6 @@
     def node_peer(t):
         i = lax.rem(at.i + t, n_nodes)
         return i, (i, at.j)
-
-    def y_peer(t):
-        y = lax.rem(at.y + t, ny)
-        return y, (at.node(y, at.xl), at.j)
 
     def z_peer(t):
         k = lax.div(nz - 1 - t, 2) + lax.rem(nz - 1 - t, 2)
@@ -200,48 +196,57 @@
         y_start(0, d, 1)
     sent_over = [sibling_copy(0, at.z, c_ref)]
     sent_over[0].start()
+    def y_arrive(s, t):
+        for d in (0, 1):
+            if t <= last_y(s, d):
+                gy_copy(s, d, t, origin(at.y, ny, d, t)).wait_recv()
+                if t < last_y(s, d):
+                    y_start(s, d, t + 1)
+
+    def z_arrive(s, d, t):
+        origin_z = origin(at.z, nz, d, t)
+        gz_copy(s, d, t, origin_z).wait_recv()
+        if t < last_z(s, d):
+            z_start(s, d, t + 1)
+        return sibling_copy(s, origin_z)
+
+    ways = [(s, d) for s in (0, 1) for d in (0, 1)]
+
+    def order(count):
+        steps = [(0, 1), (0, 2)]
+        for t in range(1, count + 1):
+            steps += [(1, t), (0, t + 2)]
+        return [(s, t) for s, t in steps if t <= count]
+
+    z_order = [(s, d, t) for s, t in order(half_z) for d in (0, 1) if t <= last_z(s, d)]
+    y_order = order(half_y)
+
+    def z_next(count):
+        over = [z_arrive(*z_order.pop(0)) for _ in range(min(count, len(z_order)))]
+        for copy in over:
+            copy.start()
+        sent_over.extend(over)
+
+    z_next(2)
+    y_arrive(*y_order.pop(0))
+    across_copy(1 - at.xh).wait_recv()
+    for d in (0, 1):
+        z_start(1, d, 1)
+    partners = sibling_copy(1, at.z)
+    partners.start()
+    sent_over.append(partners)
+    beside_copy(1 - at.xl).wait_recv()
+    for d in (0, 1):
+        y_start(1, d, 1)
     for load in loads:
         load.wait()
     spread_chains(rows, cols, live[0], n_feat, n_nodes, row_mat, col_mat, chain)
     chain_copy = pltpu.make_async_copy(chain.at[pl.ds(0, slots)], index, load_sem.at[0])
     chain_copy.start()
-    beside_copy(1 - at.xl).wait_recv()
-    for d in (0, 1):
-        y_start(1, d, 1)
-    across_copy(1 - at.xh).wait_recv()
-    for d in (0, 1):
-        z_start(1, d, 1)
-    copy = sibling_copy(1, at.z)
-    copy.start()
-    sent_over.append(copy)
-
-
-    def y_arrive(t):
-        for s in (0, 1):
-            for d in (0, 1):
-                if t <= last_y(s, d):
-                    gy_copy(s, d, t, origin(at.y, ny, d, t)).wait_recv()
-                    if t < last_y(s, d):
-                        y_start(s, d, t + 1)
-
-    def z_arrive(s, d, t):
-        if t <= last_z(s, d):
-            origin_z = origin(at.z, nz, d, t)
-            gz_copy(s, d, t, origin_z).wait_recv()
-            if t < last_z(s, d):
-                z_start(s, d, t + 1)
-            over = sibling_copy(s, origin_z)
-            over.start()
-            sent_over.append(over)
-
-    ways = [(s, d) for s in (0, 1) for d in (0, 1)]
-    split = max(1, half_z - 2)
-    for t in range(1, max(split, half_y) + 1):
-        if t <= half_y:
-            y_arrive(t)
-        if t <= split:
-            for s, d in ways:
-                z_arrive(s, d, t)
+    while y_order:
+        if len(y_order) > 1:
+            z_next(2)
+        y_arrive(*y_order.pop(0))
 
     def add_chain(sums, terms, before, k0):
         for u, term in enumerate(terms):
@@ -276,14 +281,10 @@
     groups = slots // GROUP
     tile_copy.wait()
     chain_copy.wait()
-    done = 0
-    rest = [(s, d, t) for t in range(split + 1, half_z) for s, d in ways]
-    for n, (s, d, t) in enumerate(rest):
-        z_arrive(s, d, t)
-        upto = groups * (n + 1) // len(rest)
-        loop(done, upto, ahead_step)
-        done = upto
-    loop(done, groups, ahead_step)
+    parts = 2
+    for part in range(parts):
+        z_next(1)
+        loop(groups * part // parts, groups * (part + 1) // parts, ahead_step)
 
     def c_copy(xh, z):
         slot = xh * nz + z
@@ -293,12 +294,11 @@
         p_tx[xh * nz + z] = own_p(xh, z, 1 - at.core).astype(jnp.bfloat16)
         c_copy(xh, z).start()
 
-    loop(0, nz - 1, lambda t: c_step(1 - at.xh, z_peer(t)[0]))
+    for part in range(parts):
+        first, end = nz * part // parts, nz * (part + 1) // parts
+        loop(first, min(end, nz - 1), lambda t: c_step(1 - at.xh, z_peer(t)[0]))
+        z_next(1)
     c_step(1 - at.xh, at.z)
-    for s, d in ways:
-        z_arrive(s, d, half_z)
-    loop(0, nz - 1, lambda t: c_step(at.xh, z_peer(t)[0]))
-    c_step(at.xh, at.z)
 
     def x_copy(z):
         return remote(x_tx.at[z], x_rx.at[z], xs.at[z], xr.at[z], across)
@@ -308,19 +308,30 @@
         x_tx[z] = (own_p(1 - at.xh, z, at.core) + wide(c_rx[(1 - at.xh) * nz + z])).astype(jnp.bfloat16)
         x_copy(z).start()
 
-    loop(0, nz - 1, lambda t: x_step(z_peer(t)[0]))
+    parts = len(z_order)
+    for part in range(parts):
+        first, end = nz * part // parts, nz * (part + 1) // parts
+        loop(first, min(end, nz - 1), lambda t: x_step(z_peer(t)[0]))
+        z_next(1)
     x_step(at.z)
+    loop(0, nz - 1, lambda t: c_step(at.xh, z_peer(t)[0]))
+    c_step(at.xh, at.z)
 
     for s in (0, 1):
         for z in range(nz):
             sibling_copy(s, z, arriving=True).wait_recv()
     loop(0, groups, back_step)
-    total = None
-    for i in range(n_nodes):
-        b_tx[i] = own_b(i // PAIR, i % PAIR).astype(jnp.bfloat16)
-        term = lax.dot_general(x_all[i], b_tx[i], (((0,), (0,)), ((), ())), preferred_element_type=jnp.float32)
-        total = term if total is None else total + term
-    w0[...] = total.astype(w0.dtype).reshape(w0.shape)
+
+    def round_b(t):
+        b_all[t] = own_b(lax.div(t, PAIR), lax.rem(t, PAIR)).astype(jnp.bfloat16)
+
+    loop(0, n_nodes, round_b)
+    width = x_all.shape[-1]
+    term = lax.dot_general(
+        x_all[...].reshape(-1, width), b_all[...].reshape(-1, width), (((0,), (0,)), ((), ())),
+        preferred_element_type=jnp.float32,
+    )
+    w0[...] = term.astype(w0.dtype).reshape(w0.shape)
 
     def w1_copy(t):
         i, device = node_peer(t)
@@ -328,28 +339,62 @@
 
     loop(1, n_nodes, lambda t: w1_copy(t).start())
 
-    def y_copy(t):
-        y, device = y_peer(t)
-        return remote(b_tx.at[pl.ds(y * PAIR, PAIR)], y_rx.at[at.y], ys.at[y], yr.at[at.y], device)
-
-    loop(1, ny, lambda t: y_copy(t).start())
-
-    def z_copy(t):
-        z, device = z_peer(t)
-        return remote(z_tx.at[z], z_rx.at[at.z], zs.at[z], zr.at[at.z], device)
+    def y_hops(d, s):
+        return half_y if d == s else ny - 1 - half_y
+
+    def ry_copy(d, s, h):
+        return remote(ry_tx.at[d, s, h - 1], ry_rx.at[d, s, h - 1], rys.at[d, s, h - 1], ryr.at[d, s, h - 1], along_y[d])
+
+    def y_hop(h):
+        for d, s in ways:
+            hops = y_hops(d, s)
+            if h <= hops:
+                value = own_b(origin(at.y, ny, 1 - d, hops + 1 - h), xl_of(s))
+                if h > 1:
+                    ry_copy(d, s, h - 1).wait_recv()
+                    value = value + wide(ry_rx[d, s, h - 2])
+                ry_tx[d, s, h - 1] = value.astype(jnp.bfloat16)
+                ry_copy(d, s, h).start()
+
+    def y_sum(s):
+        value = own_b(at.y, xl_of(s))
+        for d in (0, 1):
+            hops = y_hops(d, s)
+            ry_copy(d, s, hops).wait_recv()
+            value = value + wide(ry_rx[d, s, hops - 1])
+        return value
+
+    z_hops = (half_z, nz - 1 - half_z)
+
+    def rz_refs(d, h):
+        late = h - (z_hops[d] - 1)
+        return (rz_tx32.at[d, late], rz_rx32.at[d, late]) if late >= 0 else (rz_tx.at[d, h - 1], rz_rx.at[d, h - 1])
+
+    def rz_copy(d, h):
+        return remote(*rz_refs(d, h), rzs.at[d, h - 1], rzr.at[d, h - 1], along_z[d])
 
     def four_sum(z):
         c_copy(at.xh, z).wait_recv()
         x_copy(z).wait_recv()
         return own_p(at.xh, z, at.core) + wide(c_rx[at.xh * nz + z]) + wide(x_rx[z])
 
-    def z_step(t):
-        z = z_peer(t)[0]
-        z_tx[z] = four_sum(z).astype(jnp.bfloat16)
-        z_copy(t).start()
-
-    first, second = nz // 3, 2 * nz // 3
-    loop(0, first, z_step)
+    def z_hop(h):
+        for d in (0, 1):
+            hops = z_hops[d]
+            if h <= hops:
+                value = four_sum(origin(at.z, nz, 1 - d, hops + 1 - h))
+                if h > 1:
+                    rz_copy(d, h - 1).wait_recv()
+                    value = value + wide(rz_refs(d, h - 1)[1][...])
+                tx = rz_refs(d, h)[0]
+                tx[...] = value.astype(tx.dtype)
+                rz_copy(d, h).start()
+
+    y_hop(1)
+    z_hop(1)
+    z_hop(2)
+    y_hop(2)
+    z_hop(3)
 
     def w1_arrival(t):
         i, device = node_peer(t)
@@ -358,11 +403,7 @@
     w1[at.i] = w0[at.i]
     loop(1, n_nodes, w1_arrival)
     me4 = at.xh * 2 + at.core
-    shared = jnp.sum(wide(w1[...]), axis=0)
-    for slot in range(4):
-        row, column = slot // 2 * 8, slot % 2 * 128
-        w4_tx[slot] = shared[row : row + 8, column : column + 128]
-    w4[me4] = w4_tx[me4]
+    w4[me4] = jnp.sum(wide(w1[...]), axis=0)
     four = [
         (at.xh * 2 + 1 - at.core, sibling),
         ((1 - at.xh) * 2 + at.core, across),
@@ -370,75 +411,50 @@
     ]
 
     def w4_copy(slot, device):
-        return remote(w4_tx.at[slot], w4.at[me4], w4s.at[slot], w4r.at[me4], device)
+        return remote(w4.at[me4], w4.at[me4], w4s.at[slot], w4r.at[me4], device)
 
     for slot, device in four:
         w4_copy(slot, device).start()
-    loop(first, second, z_step)
+    z_hop(4)
+    y_hop(3)
 
     for slot, device in four:
-        remote(w4_tx.at[slot], w4.at[slot], w4s.at[slot], w4r.at[slot], device).wait_recv()
-    wz[at.z] = jnp.sum(w4[...], axis=0)
+        remote(w4.at[slot], w4.at[slot], w4s.at[slot], w4r.at[slot], device).wait_recv()
+    wz[at.z] = jnp.sum(w4[...], axis=0).astype(wz.dtype)
 
     def wz_copy(t):
         z, device = z_peer(t)
         return remote(wz.at[at.z], wz.at[at.z], wzs.at[z], wzr.at[at.z], device)
 
     loop(0, nz - 1, lambda t: wz_copy(t).start())
-    loop(second, nz - 1, z_step)
-    mine = four_sum(at.z)
+    z_hop(5)
+    y_hop(4)
+    z_hop(6)
 
     def wz_arrival(t):
         z, device = z_peer(t)
         remote(wz.at[z], wz.at[z], wzs.at[z], wzr.at[z], device).wait_recv()
 
     loop(0, nz - 1, wz_arrival)
-    w5[me4] = jnp.sum(wz[...], axis=0) * scale
-
-    def w5_copy(slot, device):
-        return remote(w5.at[me4], w5.at[me4], w5s.at[slot], w5r.at[me4], device)
-
-    for slot, device in four:
-        w5_copy(slot, device).start()
-    for slot, device in four:
-        remote(w5.at[slot], w5.at[slot], w5s.at[slot], w5r.at[slot], device).wait_recv()
-    wn[at.i] = jnp.concatenate(
-        [jnp.concatenate([w5[2 * half], w5[2 * half + 1]], axis=1) for half in (0, 1)], axis=0
-    ).astype(wn.dtype)
+    wn[at.i] = (jnp.sum(wide(wz[...]), axis=0) * scale).astype(wn.dtype)
 
     def wn_copy(t):
         i, device = node_peer(t)
         return remote(wn.at[at.i], wn.at[at.i], wns.at[i], wnr.at[at.i], device)
 
     loop(1, n_nodes, lambda t: wn_copy(t).start())
-
-    def y_arrival(t):
-        y, device = y_peer(t)
-        remote(b_tx.at[pl.ds(y * PAIR, PAIR)], y_rx.at[y], ys.at[y], yr.at[y], device).wait_recv()
-
-    loop(1, ny, y_arrival)
-
-    def y_sum(xl):
-        def add(t, total):
-            return total + wide(y_rx[y_peer(t)[0], xl])
-
-        return lax.fori_loop(1, ny, add, own_b(at.y, xl))
-
     l_copy = remote(l_tx, l_rx, ls, lr, beside)
-    l_tx[...] = y_sum(1 - at.xl).astype(jnp.bfloat16)
+    l_tx[...] = y_sum(1).astype(jnp.bfloat16)
     l_copy.start()
-    near = y_sum(at.xl)
-
-    def z_arrival(t, total):
-        z, device = z_peer(t)
-        remote(z_tx.at[z], z_rx.at[z], zs.at[z], zr.at[z], device).wait_recv()
-        return total + wide(z_rx[z])
-
-    whole = lax.fori_loop(0, nz - 1, z_arrival, mine)
-    out_ref[...] = split_dot(whole, weight_ref[...], ((1,), (0,))).astype(out_ref.dtype)
-
+    near = y_sum(0)
     l_copy.wait_recv()
     fg_ref[...] = split_dot(near + wide(l_rx[...]), weight_ref[...], ((1,), (1,))).astype(fg_ref.dtype)
+
+    whole = four_sum(at.z)
+    for d in (0, 1):
+        rz_copy(d, z_hops[d]).wait_recv()
+        whole = whole + wide(rz_refs(d, z_hops[d])[1][...])
+    out_ref[...] = split_dot(whole, weight_ref[...], ((1,), (0,))).astype(out_ref.dtype)
 
     def wn_arrival(t):
         i, device = node_peer(t)
@@ -455,11 +471,14 @@
         loop(0, nz, lambda z: c_copy(xh, z).wait_send())
     loop(0, nz, lambda z: x_copy(z).wait_send())
     loop(1, n_nodes, lambda t: w1_copy(t).wait_send())
-    loop(1, ny, lambda t: y_copy(t).wait_send())
-    loop(0, nz - 1, lambda t: z_copy(t).wait_send())
+    for d, s in ways:
+        for h in range(1, y_hops(d, s) + 1):
+            ry_copy(d, s, h).wait_send()
+    for d in (0, 1):
+        for h in range(1, z_hops[d] + 1):
+            rz_copy(d, h).wait_send()
     for slot, device in four:
         w4_copy(slot, device).wait_send()
-        w5_copy(slot, device).wait_send()
     loop(0, nz - 1, lambda t: wz_copy(t).wait_send())
     l_copy.wait_send()
     loop(1, n_nodes, lambda t: wn_copy(t).wait_send())
@@ -478,9 +497,6 @@
 
     def shares(count, kind):
         return pltpu.VMEM((count, share, width), kind)
-
-    def pieces(count):
-        return pltpu.VMEM((count, share // 2, width // 2), jnp.float32)
 
     def pairs(*counts):
         return [sem for count in counts for sem in [dma(count) if count else dma] * 2]
@@ -509,28 +525,29 @@
             blocks(slots, kind=jnp.float32),
             blocks(slots, kind=jnp.float32),
             blocks(2 * nz),
-            blocks(n_nodes),
             blocks(2 * nz),
             blocks(nz),
             blocks(nz),
-            blocks(nz),
-            blocks(nz),
-            blocks(ny, PAIR),
+            blocks(2, nz // 2),
+            blocks(2, nz // 2),
+            blocks(2, 2, kind=jnp.float32),
+            blocks(2, 2, kind=jnp.float32),
+            blocks(2, 2, ny // 2),
+            blocks(2, 2, ny // 2),
             blocks(),
             blocks(),
+            blocks(n_nodes),
             shares(n_nodes, jnp.bfloat16),
             shares(n_nodes, jnp.bfloat16),
-            pieces(4),
-            pieces(4),
-            pieces(nz),
-            pieces(4),
+            shares(4, jnp.float32),
+            shares(nz, jnp.bfloat16),
             shares(n_nodes, jnp.bfloat16),
             dma((6,)),
             dma,
         ]
         + pairs(None, (2, 2, nz // 2), (2 * nz,), None, (2, 2, ny // 2))
-        + pairs((2 * nz,), (nz,), (nz,), (ny,), None)
-        + pairs((n_nodes,), (4,), (nz,), (4,), (n_nodes,)),
+        + pairs((2 * nz,), (nz,), (2, nz // 2), (2, 2, ny // 2), None)
+        + pairs((n_nodes,), (4,), (nz,), (n_nodes,)),
         compiler_params=pltpu.CompilerParams(collective_id=0, has_side_effects=True, vmem_limit_bytes=LIMIT),
         name="graph_layer",
     )(tile_rows, tile_cols, live, features, cotangent, weight, tiles)

time: 102 us -> 92.5 us (0.907)
  Pallas kernels: 95.5 us -> 85.7 us
    pallas_call x1, Pallas kernels: 95.5 us -> 85.7 us  [body(): pl.pallas_call(functools.partial(kernel, n_nodes, n_feat, scale), out_sha...]
where the time goes in v4:
time: 92.5 us; the launch traced here: 91.6 us
  Pallas kernels  85.7 us (93%)
  local copies, waits for them, and re-layouts  4.61 us (5%)
  between operations  1.29 us (1%)
    pallas_call x1, Pallas kernels, body(): pl.pallas_call(functools.partial(kernel, n_nodes, n_feat, scale), out_sha...  85.7 us
    unnamed x3, local copies, waits for them, and re-layouts  4.61 us

profile of v4, /device:TPU:1, one launch (start us, length us, event | category | flops | bytes accessed | tf_op | source)
XLA Modules:
  0.0 91.6 jit_solution(5722154585361531866)
XLA Ops:
  1.3 85.7 %graph_layer.1 = (bf16[128,256]{1,0:T(8,128)(2,1)}, bf16[128,256]{1,0:T(8,128)(2,1)}, f32[16,16,256]{2,1,0:T(8,128)}) custom-call(s32[48]{0:T(128)} %rows_ref.1, s32[48]{0:T(128)} %cols_ref.1, s32[1]{0:T(128)S(6)} %copy.13.live_ref, bf16[128,256]{1,0:T(8,128)(2,1)} %x_ref.1, bf16[128,256]{1,0:T(8,128)(2,1)} %c_ref.1, bf16[256,256]{1,0:T(8,128)(2,1)} %weight_in.1, ...), custom_call_target="tpu_custom_call" | custom-call | tf_op jit(solution)/shard_map/graph_layer/pallas_call | solution.py:504
  87.0 1.5 %copy.14 = bf16[128,256]{1,0:T(8,128)(2,1)} copy(bf16[128,256]{1,0:T(8,128)(2,1)} %get-tuple-element.12) | data formatting | bytes 131072
  88.5 1.5 %copy.15 = bf16[128,256]{1,0:T(8,128)(2,1)} copy(bf16[128,256]{1,0:T(8,128)(2,1)} %get-tuple-element.13) | data formatting | bytes 131072
  90.0 1.7 %copy.16 = f32[256,256]{1,0:T(8,128)} copy(f32[256,256]{1,0:T(8,128)} %bitcast.1) | data formatting | bytes 524288

commit v5 on v4

--- a/solution.py
+++ b/solution.py
@@ -13,7 +13,7 @@
 ANY = pl.BlockSpec(memory_space=pl.ANY)
 LIMIT = 60 * 1024 * 1024
 LANES = 128
-GROUP = 4
+GROUP = 16
 PAIR = 2
 
 
@@ -443,25 +443,6 @@
         return remote(wn.at[at.i], wn.at[at.i], wns.at[i], wnr.at[at.i], device)
 
     loop(1, n_nodes, lambda t: wn_copy(t).start())
-    l_copy = remote(l_tx, l_rx, ls, lr, beside)
-    l_tx[...] = y_sum(1).astype(jnp.bfloat16)
-    l_copy.start()
-    near = y_sum(0)
-    l_copy.wait_recv()
-    fg_ref[...] = split_dot(near + wide(l_rx[...]), weight_ref[...], ((1,), (1,))).astype(fg_ref.dtype)
-
-    whole = four_sum(at.z)
-    for d in (0, 1):
-        rz_copy(d, z_hops[d]).wait_recv()
-        whole = whole + wide(rz_refs(d, z_hops[d])[1][...])
-    out_ref[...] = split_dot(whole, weight_ref[...], ((1,), (0,))).astype(out_ref.dtype)
-
-    def wn_arrival(t):
-        i, device = node_peer(t)
-        remote(wn.at[i], wn.at[i], wns.at[i], wnr.at[i], device).wait_recv()
-
-    loop(1, n_nodes, wn_arrival)
-    wg_ref[...] = wide(wn[...])
 
     for sent in sent_over + z_sent + y_sent:
         sent.wait_send()
@@ -471,6 +452,26 @@
         loop(0, nz, lambda z: c_copy(xh, z).wait_send())
     loop(0, nz, lambda z: x_copy(z).wait_send())
     loop(1, n_nodes, lambda t: w1_copy(t).wait_send())
+    l_copy = remote(l_tx, l_rx, ls, lr, beside)
+    l_tx[...] = y_sum(1).astype(jnp.bfloat16)
+    l_copy.start()
+    near = y_sum(0)
+    l_copy.wait_recv()
+    fg_ref[...] = split_dot(near + wide(l_rx[...]), weight_ref[...], ((1,), (1,))).astype(fg_ref.dtype)
+
+    whole = four_sum(at.z)
+    for d in (0, 1):
+        rz_copy(d, z_hops[d]).wait_recv()
+        whole = whole + wide(rz_refs(d, z_hops[d])[1][...])
+    out_ref[...] = split_dot(whole, weight_ref[...], ((1,), (0,))).astype(out_ref.dtype)
+
+    def wn_arrival(t):
+        i, device = node_peer(t)
+        remote(wn.at[i], wn.at[i], wns.at[i], wnr.at[i], device).wait_recv()
+
+    loop(1, n_nodes, wn_arrival)
+    wg_ref[...] = wide(wn[...])
+
     for d, s in ways:
         for h in range(1, y_hops(d, s) + 1):
             ry_copy(d, s, h).wait_send()

time: 92.5 us -> 90.3 us (0.976)
  Pallas kernels: 85.7 us -> 84.1 us
    pallas_call x1, Pallas kernels: 85.7 us -> 84.1 us  [body(): pl.pallas_call(functools.partial(kernel, n_nodes, n_feat, scale), out_sha...]
where the time goes in v5:
time: 90.3 us; the launch traced here: 90 us
  Pallas kernels  84.1 us (93%)
  local copies, waits for them, and re-layouts  4.61 us (5%)
  between operations  1.29 us (1%)
    pallas_call x1, Pallas kernels, body(): pl.pallas_call(functools.partial(kernel, n_nodes, n_feat, scale), out_sha...  84.1 us
    unnamed x3, local copies, waits for them, and re-layouts  4.61 us

profile of v5, /device:TPU:1, one launch (start us, length us, event | category | flops | bytes accessed | tf_op | source)
XLA Modules:
  0.0 90.0 jit_solution(335558470962766082)
XLA Ops:
  1.3 84.1 %graph_layer.1 = (bf16[128,256]{1,0:T(8,128)(2,1)}, bf16[128,256]{1,0:T(8,128)(2,1)}, f32[16,16,256]{2,1,0:T(8,128)}) custom-call(s32[48]{0:T(128)} %rows_ref.1, s32[48]{0:T(128)} %cols_ref.1, s32[1]{0:T(128)S(6)} %copy.13.live_ref, bf16[128,256]{1,0:T(8,128)(2,1)} %x_ref.1, bf16[128,256]{1,0:T(8,128)(2,1)} %c_ref.1, bf16[256,256]{1,0:T(8,128)(2,1)} %weight_in.1, ...), custom_call_target="tpu_custom_call" | custom-call | tf_op jit(solution)/shard_map/graph_layer/pallas_call | solution.py:505
  85.4 1.5 %copy.14 = bf16[128,256]{1,0:T(8,128)(2,1)} copy(bf16[128,256]{1,0:T(8,128)(2,1)} %get-tuple-element.12) | data formatting | bytes 131072
  86.9 1.5 %copy.15 = bf16[128,256]{1,0:T(8,128)(2,1)} copy(bf16[128,256]{1,0:T(8,128)(2,1)} %get-tuple-element.13) | data formatting | bytes 131072
  88.3 1.7 %copy.16 = f32[256,256]{1,0:T(8,128)} copy(f32[256,256]{1,0:T(8,128)} %bitcast.1) | data formatting | bytes 524288
